TPU v7x, 32 devices: a whole 2x2x4 slice. The times are simulated.
32 devices in a mesh: batch: 2 (over y), tm: 4 (over z), height: 4 (over x, core).
Axes of the slice: x: 2, y: 2, z: 4, core: 2. Of those that a mesh axis runs over, the one named last changes fastest.
Arguments:
- features: bfloat16 [2, 8, 32, 128, 128], P('batch', 'tm', 'height'), may hold values from -6 to 6
- w_spatial: bfloat16 [3, 3, 128, 128], replicated, may hold values from -0.1875 to 0.1875
- w_temporal: bfloat16 [3, 128, 128], replicated, may hold values from -0.3125 to 0.3125
- w_down: bfloat16 [3, 128, 128], replicated, may hold values from -0.3125 to 0.3125
- cotangent: bfloat16 [2, 4, 32, 128, 128], P('batch', 'tm', 'height'), may hold values from -40 to 40
Outputs:
- downsampled: bfloat16 [2, 4, 32, 128, 128], P('batch', 'tm', 'height')
- grad_features: bfloat16 [2, 8, 32, 128, 128], P('batch', 'tm', 'height')
- grad_spatial: float32 [3, 3, 128, 128], replicated
- grad_temporal: float32 [3, 128, 128], replicated
- grad_down: float32 [3, 128, 128], replicated
All inputs are finite; a program needn't handle non-finite values.
Results may differ from a plain program's by a relative error of at most 0.0052.
Values may be sent and summed in bfloat16 or wider, within the bound.
A program may use at most 64 MiB of HBM per device.

v0:
```python
import jax
import jax.numpy as jnp
from jax import lax
from jax.sharding import PartitionSpec as P


def with_halo(block, sides, width):
    for axis, dim in sides:
        count = lax.axis_size(axis)
        forward = [(i, i + 1) for i in range(count - 1)]
        backward = [(target, source) for source, target in forward]
        low = lax.ppermute(
            lax.slice_in_dim(block, block.shape[dim] - width, None, axis=dim), axis, forward
        )
        high = lax.ppermute(lax.slice_in_dim(block, 0, width, axis=dim), axis, backward)
        block = jnp.concatenate([low, block, high], axis=dim)
    return block


def from_behind(shard, axis, by):
    count = lax.axis_size(axis)
    pairs = [(i, i + by) for i in range(count) if 0 <= i + by < count]
    return lax.ppermute(shard, axis, pairs)


def spatial(padded, kernel):
    rows = padded.shape[2] - 2
    cols = padded.shape[3]
    wide = jnp.pad(padded, ((0, 0), (0, 0), (0, 0), (1, 1), (0, 0)))
    total = jnp.zeros(padded.shape[:2] + (rows, cols, kernel.shape[3]), jnp.float32)
    for dy in range(3):
        for dx in range(3):
            total = total + jnp.einsum(
                "bfhwc,cd->bfhwd",
                wide[:, :, dy : dy + rows, dx : dx + cols],
                kernel[dy, dx],
                preferred_element_type=jnp.float32,
            )
    return total


def spatial_grad(padded, grad):
    rows = grad.shape[2]
    cols = grad.shape[3]
    wide = jnp.pad(padded, ((0, 0), (0, 0), (0, 0), (1, 1), (0, 0)))
    taps = []
    for dy in range(3):
        for dx in range(3):
            taps.append(
                jnp.einsum(
                    "bfhwc,bfhwd->cd",
                    wide[:, :, dy : dy + rows, dx : dx + cols],
                    grad,
                    preferred_element_type=jnp.float32,
                )
            )
    return jnp.stack(taps).reshape(3, 3, grad.shape[4], grad.shape[4])


def temporal(padded, kernel):
    frames = padded.shape[1] - 2
    total = jnp.zeros(
        padded.shape[:1] + (frames,) + padded.shape[2:4] + (kernel.shape[2],), jnp.float32
    )
    for k in range(3):
        total = total + jnp.einsum(
            "bfhwc,cd->bfhwd",
            padded[:, k : k + frames],
            kernel[k],
            preferred_element_type=jnp.float32,
        )
    return total


def per_device(features, w_spatial, w_temporal, w_down, cotangent):
    frames = features.shape[1]
    half = cotangent.shape[1]
    xpad = with_halo(features, (("height", 2),), 1)
    pre = spatial(xpad, w_spatial)
    act = jax.nn.silu(pre).astype(jnp.bfloat16)
    act_pad = with_halo(act, (("tm", 1),), 1)
    mixed = temporal(act_pad, w_temporal)
    resid = (features.astype(jnp.float32) + mixed).astype(jnp.bfloat16)
    before = from_behind(resid[:, -1:], "tm", 1)
    rpad = jnp.concatenate([before, resid], axis=1)
    down = jnp.zeros(cotangent.shape, jnp.float32)
    grad_down = []
    for k in range(3):
        picked = rpad[:, k : k + 2 * half : 2]
        down = down + jnp.einsum(
            "bfhwc,cd->bfhwd", picked, w_down[k], preferred_element_type=jnp.float32
        )
        grad_down.append(
            jnp.einsum("bfhwc,bfhwd->cd", picked, cotangent, preferred_element_type=jnp.float32)
        )
    grad_down = jnp.stack(grad_down)
    downsampled = down.astype(jnp.bfloat16)
    after = from_behind(cotangent, "tm", -1)
    gnext = jnp.concatenate([cotangent[:, 1:], after], axis=1)
    even = jnp.einsum("bfhwd,cd->bfhwc", cotangent, w_down[1], preferred_element_type=jnp.float32)
    odd = jnp.einsum("bfhwd,cd->bfhwc", cotangent, w_down[2], preferred_element_type=jnp.float32)
    odd = odd + jnp.einsum("bfhwd,cd->bfhwc", gnext, w_down[0], preferred_element_type=jnp.float32)
    g_resid = jnp.stack([even, odd], axis=2).reshape(features.shape)
    g_resid_b = g_resid.astype(jnp.bfloat16)
    gpad = with_halo(g_resid_b, (("tm", 1),), 1)
    flip_t = jnp.transpose(w_temporal[::-1], (0, 2, 1))
    g_act = temporal(gpad, flip_t)
    grad_temporal = jnp.stack(
        [
            jnp.einsum(
                "bfhwc,bfhwd->cd",
                act_pad[:, k : k + frames],
                g_resid_b,
                preferred_element_type=jnp.float32,
            )
            for k in range(3)
        ]
    )
    sig = jax.nn.sigmoid(pre)
    g_pre = (g_act * sig * (1.0 + pre * (1.0 - sig))).astype(jnp.bfloat16)
    grad_spatial = spatial_grad(xpad, g_pre)
    g_prepad = with_halo(g_pre, (("height", 2),), 1)
    flip_s = jnp.transpose(w_spatial[::-1, ::-1], (0, 1, 3, 2))
    grad_features = (g_resid + spatial(g_prepad, flip_s)).astype(jnp.bfloat16)
    grad_spatial, grad_temporal, grad_down = lax.psum(
        (grad_spatial, grad_temporal, grad_down), ("batch", "tm", "height")
    )
    return (downsampled, grad_features, grad_spatial, grad_temporal, grad_down)


def solution(mesh):
    placed = (
        P("batch", "tm", "height", None, None),
        P(),
        P(),
        P(),
        P("batch", "tm", "height", None, None),
    )
    return jax.shard_map(
        per_device,
        mesh=mesh,
        in_specs=placed,
        out_specs=(
            P("batch", "tm", "height", None, None),
            P("batch", "tm", "height", None, None),
            P(),
            P(),
            P(),
        ),
        check_vma=False,
    )
```

profile of v0, /device:TPU:0, one launch (start us, length us, event | category | flops | bytes accessed | tf_op | source)
XLA Modules:
  0.0 202.0 jit_solution(9419475674199242681)
XLA Ops:
  7.2 0.9 fusion.130
  8.2 2.4 %collective-permute-start = (bf16[1,2,1,128,128]{4,3,2,1,0:T(8,128)(2,1)S(1)}, bf16[1,2,1,128,128]{4,3,2,1,0:T(8,128)(2,1)S(1)}, u32[]{:S(2)}, u32[]{:S(2)}) collective-permute-start(bf16[1,2,1,128,128]{4,3,2,1,0:T(8,128)(2,1)S(1)} %get-tuple-element.14), channel_id=1, source_target_pairs={{0,1},{1,2},{2,3},{4,5},{5,6},{6,7},{8,9},{9,10},{10,11},{12,13},{... | collective-permute-start | bytes 196616 | tf_op jit(solution)/shard_map/ppermute | solution.py:12
  10.6 1.4 collective-permute-start.1
  12.0 1.3 collective-permute-start.5
  13.3 1.2 fusion.60
  14.7 0.7 convert_bitcast_fusion.1
  16.4 0.3 fusion.51
  17.0 0.3 convolution_add_fusion.14
  18.5 0.5 multiply_convert_fusion
  19.0 1.3 collective-permute-start.3
  20.3 5.6 %collective-permute-start.2 = (bf16[1,1,8,128,128]{4,3,2,1,0:T(8,128)(2,1)S(1)}, bf16[1,1,8,128,128]{4,3,2,1,0:T(8,128)(2,1)S(1)}, u32[]{:S(2)}, u32[]{:S(2)}) collective-permute-start(bf16[1,1,8,128,128]{4,3,2,1,0:T(8,128)(2,1)S(1)} %get-tuple-element.12), channel_id=1, source_target_pairs={{0,4},{4,8},{8,12},{1,5},{5,9},{9,13},{2,6},{6,10},{10,14},{3,7},{... | collective-permute-start | bytes 786440 | tf_op jit(solution)/shard_map/ppermute | solution.py:12
  26.2 1.2 convolution_add_fusion.16
  27.5 0.8 copy-done.4
  28.7 0.3 convolution_bitcast_fusion.1
  29.0 1.3 collective-permute-start.7
  30.3 4.6 %collective-permute-start.6 = (bf16[1,1,8,128,128]{4,3,2,1,0:T(8,128)(2,1)S(1)}, bf16[1,1,8,128,128]{4,3,2,1,0:T(8,128)(2,1)S(1)}, u32[]{:S(2)}, u32[]{:S(2)}) collective-permute-start(bf16[1,1,8,128,128]{4,3,2,1,0:T(8,128)(2,1)S(1)} %get-tuple-element.10), channel_id=1, source_target_pairs={{0,4},{4,8},{8,12},{1,5},{5,9},{9,13},{2,6},{6,10},{10,14},{3,7},{... | collective-permute-start | bytes 786440 | tf_op jit(solution)/shard_map/ppermute | solution.py:12
  35.2 0.3 fusion.11
  36.1 1.0 fusion.69
  37.1 3.9 %collective-permute-start.4 = (bf16[1,1,8,128,128]{4,3,2,1,0:T(8,128)(2,1)S(1)}, bf16[1,1,8,128,128]{4,3,2,1,0:T(8,128)(2,1)S(1)}, u32[]{:S(2)}, u32[]{:S(2)}) collective-permute-start(bf16[1,1,8,128,128]{4,3,2,1,0:T(8,128)(2,1)S(1)} %slice.271), channel_id=1, source_target_pairs={{0,4},{4,8},{8,12},{1,5},{5,9},{9,13},{2,6},{6,10},{10,14},{3,7},{... | collective-permute-start | bytes 786440 | tf_op jit(solution)/shard_map/ppermute | solution.py:23
  41.0 0.3 convolution_bitcast_fusion
  41.3 0.4 convolution_bitcast_fusion.2
  42.0 0.7 pad_maximum_fusion.10
  43.0 0.6 fusion.10
  43.6 0.3 fusion.25
  43.9 0.3 fusion.24
  44.3 0.3 fusion.23
  44.6 0.3 fusion.22
  44.9 0.4 fusion.21
  45.3 0.3 fusion.20
  45.7 0.3 fusion.19
  46.0 3.0 %collective-permute-start.8 = (bf16[1,2,1,128,128]{4,3,2,1,0:T(8,128)(2,1)S(1)}, bf16[1,2,1,128,128]{4,3,2,1,0:T(8,128)(2,1)S(1)}, u32[]{:S(2)}, u32[]{:S(2)}) collective-permute-start(bf16[1,2,1,128,128]{4,3,2,1,0:T(8,128)(2,1)S(1)} %get-tuple-element.8), channel_id=1, source_target_pairs={{0,1},{1,2},{2,3},{4,5},{5,6},{6,7},{8,9},{9,10},{10,11},{12,13},{... | collective-permute-start | bytes 196616 | tf_op jit(solution)/shard_map/ppermute | solution.py:12
  49.1 1.5 collective-permute-start.9
  50.6 0.3 fusion.18
  50.9 0.3 fusion.17
  51.3 3.9 %collective-permute-done.9 = bf16[1,2,1,128,128]{4,3,2,1,0:T(8,128)(2,1)S(1)} collective-permute-done((bf16[1,2,1,128,128]{4,3,2,1,0:T(8,128)(2,1)S(1)}, bf16[1,2,1,128,128]{4,3,2,1,0:T(8,128)(2,1)S(1)}, u32[]{:S(2)}, u32[]{:S(2)}) %collective-permute-start.9) | collective-permute-done | bytes 65568 | tf_op jit(solution)/shard_map/ppermute | solution.py:15
  55.9 0.3 convolution_add_fusion.5
  56.8 0.3 convolution_add_fusion.2
  57.1 1.3 convolution_add_fusion.1
  58.6 0.4 copy-done.5
  59.1 0.7 pad_maximum_fusion.11
  59.8 0.9 copy-done.6
  60.7 2.0 fusion.16
  63.0 0.9 copy-done.2
  63.9 1.1 fusion.13
  65.0 126.8 %all-reduce.5.cloned.1.call-done = (f32[3,3,128,128]{3,2,1,0:T(8,128)}, f32[3,128,128]{2,1,0:T(8,128)}, f32[3,128,128]{2,1,0:T(8,128)}) async-done(((f32[3,3,128,128]{3,2,1,0:T(8,128)}, f32[3,128,128]{2,1,0:T(8,128)}, f32[3,128,128]{2,1,0:T(8,128)}), (f32[3,3,128,128]{3,2,1,0:T(8,128)}, f32[3,128,128]{2,1,0:T(8,128)}, f32[3,128,128]{2,1,0:T(8,128)})) %all-reduce.5.cloned.1.call-update) | async-done | bytes 983056 | tf_op jit(solution)/shard_map/psum | solution.py:125
  191.9 2.0 copy.91
  193.8 0.7 copy.92
  194.5 0.7 copy.93
  (67 shorter events, 6.6 us)
Async XLA Ops:
  7.2 7.3 %copy-start.1 = (bf16[1,1,8,128,128]{4,3,2,1,0:T(8,128)(2,1)S(1)}, bf16[1,1,8,128,128]{4,3,2,1,0:T(8,128)(2,1)}, u32[]{:S(2)}) copy-start(bf16[1,1,8,128,128]{4,3,2,1,0:T(8,128)(2,1)} %param.9) | copy-start | bytes 786436
  7.2 7.3 %copy-start.9 = (bf16[3,128,128]{2,1,0:T(8,128)(2,1)S(1)}, bf16[3,128,128]{2,1,0:T(8,128)(2,1)}, u32[]{:S(2)}) copy-start(bf16[3,128,128]{2,1,0:T(8,128)(2,1)} %param.8) | copy-start | bytes 294916
  7.2 184.7 %all-reduce.5.cloned.1.call-start = ((), (), s32[]{:S(2)}) async-start(), calls=%async_computation | async-start | bytes 1966080 | tf_op jit(solution)/shard_map/psum | solution.py:125
  8.2 7.7 %collective-permute-start = (bf16[1,2,1,128,128]{4,3,2,1,0:T(8,128)(2,1)S(1)}, bf16[1,2,1,128,128]{4,3,2,1,0:T(8,128)(2,1)S(1)}, u32[]{:S(2)}, u32[]{:S(2)}) collective-permute-start(bf16[1,2,1,128,128]{4,3,2,1,0:T(8,128)(2,1)S(1)} %get-tuple-element.14), channel_id=1, source_target_pairs={{0,1},{1,2},{2,3},{4,5},{5,6},{6,7},{8,9},{9,10},{10,11},{12,13},{... | collective-permute-start | bytes 196616 | tf_op jit(solution)/shard_map/ppermute | solution.py:12
  10.5 4.9 %copy-start.8 = (bf16[3,128,128]{2,1,0:T(8,128)(2,1)S(1)}, bf16[3,128,128]{2,1,0:T(8,128)(2,1)}, u32[]{:S(2)}) copy-start(bf16[3,128,128]{2,1,0:T(8,128)(2,1)} %param.7) | copy-start | bytes 294916
  10.6 5.4 %collective-permute-start.1 = (bf16[1,2,1,128,128]{4,3,2,1,0:T(8,128)(2,1)S(1)}, bf16[1,2,1,128,128]{4,3,2,1,0:T(8,128)(2,1)S(1)}, u32[]{:S(2)}, u32[]{:S(2)}) collective-permute-start(bf16[1,2,1,128,128]{4,3,2,1,0:T(8,128)(2,1)S(1)} %get-tuple-element.15), channel_id=1, source_target_pairs={{1,0},{2,1},{3,2},{5,4},{6,5},{7,6},{9,8},{10,9},{11,10},{13,12},{... | collective-permute-start | bytes 196616 | tf_op jit(solution)/shard_map/ppermute | solution.py:15
  12.0 14.2 %collective-permute-start.5 = (bf16[1,1,8,128,128]{4,3,2,1,0:T(8,128)(2,1)}, bf16[1,1,8,128,128]{4,3,2,1,0:T(8,128)(2,1)}, u32[]{:S(2)}, u32[]{:S(2)}) collective-permute-start(bf16[1,1,8,128,128]{4,3,2,1,0:T(8,128)(2,1)} %param.9), channel_id=1, source_target_pairs={{4,0},{8,4},{12,8},{5,1},{9,5},{13,9},{6,2},{10,6},{14,10},{7,3},{... | collective-permute-start | bytes 786440 | tf_op jit(solution)/shard_map/ppermute | solution.py:23
  14.5 1.1 copy-start.3
  14.7 1.2 copy-start
  15.9 2.5 %copy-start.12 = (bf16[1,2,1,128,128]{4,3,2,1,0:T(8,128)(2,1)}, bf16[1,2,1,128,128]{4,3,2,1,0:T(8,128)(2,1)S(1)}, u32[]{:S(2)}) copy-start(bf16[1,2,1,128,128]{4,3,2,1,0:T(8,128)(2,1)S(1)} %collective-permute-done.1) | copy-start | bytes 196612
  19.0 15.9 %collective-permute-start.3 = (bf16[1,1,8,128,128]{4,3,2,1,0:T(8,128)(2,1)S(1)}, bf16[1,1,8,128,128]{4,3,2,1,0:T(8,128)(2,1)S(1)}, u32[]{:S(2)}, u32[]{:S(2)}) collective-permute-start(bf16[1,1,8,128,128]{4,3,2,1,0:T(8,128)(2,1)S(1)} %get-tuple-element.13), channel_id=1, source_target_pairs={{4,0},{8,4},{12,8},{5,1},{9,5},{13,9},{6,2},{10,6},{14,10},{7,3},{... | collective-permute-start | bytes 786440 | tf_op jit(solution)/shard_map/ppermute | solution.py:15
  20.3 14.9 %collective-permute-start.2 = (bf16[1,1,8,128,128]{4,3,2,1,0:T(8,128)(2,1)S(1)}, bf16[1,1,8,128,128]{4,3,2,1,0:T(8,128)(2,1)S(1)}, u32[]{:S(2)}, u32[]{:S(2)}) collective-permute-start(bf16[1,1,8,128,128]{4,3,2,1,0:T(8,128)(2,1)S(1)} %get-tuple-element.12), channel_id=1, source_target_pairs={{0,4},{4,8},{8,12},{1,5},{5,9},{9,13},{2,6},{6,10},{10,14},{3,7},{... | collective-permute-start | bytes 786440 | tf_op jit(solution)/shard_map/ppermute | solution.py:12
  27.4 1.0 copy-start.4
  29.0 13.6 %collective-permute-start.7 = (bf16[1,1,8,128,128]{4,3,2,1,0:T(8,128)(2,1)S(1)}, bf16[1,1,8,128,128]{4,3,2,1,0:T(8,128)(2,1)S(1)}, u32[]{:S(2)}, u32[]{:S(2)}) collective-permute-start(bf16[1,1,8,128,128]{4,3,2,1,0:T(8,128)(2,1)S(1)} %get-tuple-element.11), channel_id=1, source_target_pairs={{4,0},{8,4},{12,8},{5,1},{9,5},{13,9},{6,2},{10,6},{14,10},{7,3},{... | collective-permute-start | bytes 786440 | tf_op jit(solution)/shard_map/ppermute | solution.py:15
  30.3 12.6 %collective-permute-start.6 = (bf16[1,1,8,128,128]{4,3,2,1,0:T(8,128)(2,1)S(1)}, bf16[1,1,8,128,128]{4,3,2,1,0:T(8,128)(2,1)S(1)}, u32[]{:S(2)}, u32[]{:S(2)}) collective-permute-start(bf16[1,1,8,128,128]{4,3,2,1,0:T(8,128)(2,1)S(1)} %get-tuple-element.10), channel_id=1, source_target_pairs={{0,4},{4,8},{8,12},{1,5},{5,9},{9,13},{2,6},{6,10},{10,14},{3,7},{... | collective-permute-start | bytes 786440 | tf_op jit(solution)/shard_map/ppermute | solution.py:12
  37.1 21.3 %collective-permute-start.4 = (bf16[1,1,8,128,128]{4,3,2,1,0:T(8,128)(2,1)S(1)}, bf16[1,1,8,128,128]{4,3,2,1,0:T(8,128)(2,1)S(1)}, u32[]{:S(2)}, u32[]{:S(2)}) collective-permute-start(bf16[1,1,8,128,128]{4,3,2,1,0:T(8,128)(2,1)S(1)} %slice.271), channel_id=1, source_target_pairs={{0,4},{4,8},{8,12},{1,5},{5,9},{9,13},{2,6},{6,10},{10,14},{3,7},{... | collective-permute-start | bytes 786440 | tf_op jit(solution)/shard_map/ppermute | solution.py:23
  45.6 4.9 %copy-start.13 = (bf16[1,2,1,128,128]{4,3,2,1,0:T(8,128)(2,1)S(1)}, bf16[1,2,1,128,128]{4,3,2,1,0:T(8,128)(2,1)}, u32[]{:S(2)}) copy-start(bf16[1,2,1,128,128]{4,3,2,1,0:T(8,128)(2,1)} %copy-done.12) | copy-start | bytes 196612
  46.0 5.2 %collective-permute-start.8 = (bf16[1,2,1,128,128]{4,3,2,1,0:T(8,128)(2,1)S(1)}, bf16[1,2,1,128,128]{4,3,2,1,0:T(8,128)(2,1)S(1)}, u32[]{:S(2)}, u32[]{:S(2)}) collective-permute-start(bf16[1,2,1,128,128]{4,3,2,1,0:T(8,128)(2,1)S(1)} %get-tuple-element.8), channel_id=1, source_target_pairs={{0,1},{1,2},{2,3},{4,5},{5,6},{6,7},{8,9},{9,10},{10,11},{12,13},{... | collective-permute-start | bytes 196616 | tf_op jit(solution)/shard_map/ppermute | solution.py:12
  49.1 6.1 %collective-permute-start.9 = (bf16[1,2,1,128,128]{4,3,2,1,0:T(8,128)(2,1)S(1)}, bf16[1,2,1,128,128]{4,3,2,1,0:T(8,128)(2,1)S(1)}, u32[]{:S(2)}, u32[]{:S(2)}) collective-permute-start(bf16[1,2,1,128,128]{4,3,2,1,0:T(8,128)(2,1)S(1)} %get-tuple-element.9), channel_id=1, source_target_pairs={{1,0},{2,1},{3,2},{5,4},{6,5},{7,6},{9,8},{10,9},{11,10},{13,12},{... | collective-permute-start | bytes 196616 | tf_op jit(solution)/shard_map/ppermute | solution.py:15
  51.3 4.4 %copy-start.7 = (f32[9,128,128]{2,1,0:T(8,128)}, f32[9,128,128]{2,1,0:T(8,128)S(1)}, u32[]{:S(2)}) copy-start(f32[9,128,128]{2,1,0:T(8,128)S(1)} %fusion.17) | copy-start | bytes 1769476
  58.4 0.7 copy-start.5
  59.8 0.9 copy-start.6
  62.7 1.2 copy-start.2
  191.8 2.0 copy-start.11
  191.8 2.7 %copy-start.10 = (f32[3,128,128]{2,1,0:T(8,128)S(1)}, f32[3,128,128]{2,1,0:T(8,128)}, u32[]{:S(2)}) copy-start(f32[3,128,128]{2,1,0:T(8,128)} %get-tuple-element.22) | copy-start | bytes 589828
Sparse Core Ops, SparseCore 0:
  59.9 131.8 all-reduce.4
where the time goes:
time: 203 us; the launch traced here: 202 us
  waiting for transfers between devices  131 us (65%)
  starting transfers between devices  26.3 us (13%)
  matrix products  19.9 us (10%)
  between operations  14.6 us (7%)
  local copies, waits for them, and re-layouts  7.92 us (4%)
  other arithmetic  2.63 us (1%)
    psum x1, waiting for transfers between devices, per_device(): lax.psum((grad_spatial, grad_temporal, grad_down), ('batch', 'tm', 'heigh...  127 us
    ppermute x4, starting transfers between devices, with_halo(): lax.ppermute(lax.slice_in_dim(block, block.shape[dim] - width, None, axis...  15.5 us
    dot_general x18, matrix products, spatial(): jnp.einsum('bfhwc,cd->bfhwd', wide[:, :, dy:dy + rows, dx:dx + cols], ker...  7.18 us
    unnamed x33, local copies, waits for them, and re-layouts  6.83 us
    ppermute x4, starting transfers between devices, with_halo(): lax.ppermute(lax.slice_in_dim(block, 0, width, axis=dim), axis, backward)  5.48 us
    ppermute x2, starting transfers between devices, from_behind(): return lax.ppermute(shard, axis, pairs)  5.2 us
  transfers between devices with their start and end apart: 11, of which 2 were waited for; matrix products, arithmetic and copies ran while one was open for 11% of the time, Pallas kernels for 0%

commit v1 on v0

--- a/solution.py
+++ b/solution.py
@@ -1,7 +1,162 @@
+import functools
+
 import jax
 import jax.numpy as jnp
 from jax import lax
+from jax.experimental import pallas as pl
+from jax.experimental.pallas import tpu as pltpu
 from jax.sharding import PartitionSpec as P
+
+MESH = pl.DeviceIdType.MESH
+AXES = ("batch", "tm", "height")
+
+
+def rows_each(mats, peers):
+    return 16 * pl.cdiv(mats * 128, 16 * peers)
+
+
+def sum_scratch(mats, peers, depth):
+    rows = rows_each(mats, peers)
+    return [
+        pltpu.VMEM((peers * rows, 128), jnp.bfloat16),
+        pltpu.VMEM((peers * rows, 128), jnp.bfloat16),
+        pltpu.VMEM((depth * rows, 128), jnp.bfloat16),
+        pltpu.VMEM((peers * rows, 128), jnp.bfloat16),
+        pltpu.SemaphoreType.DMA((3, 2, max(peers, depth))),
+    ]
+
+
+class Sum:
+    def __init__(self, dims, mats, refs):
+        self.nb, self.nz, self.nh = dims
+        self.mats = mats
+        self.peers = self.nb * self.nh
+        self.rows = rows_each(mats, self.peers)
+        self.out, self.got, self.deep, self.full, self.sems = refs
+        self.b, self.z, self.h = (lax.axis_index(a) for a in AXES)
+        self.me = self.b * self.nh + self.h
+
+    def slot(self, i):
+        return pl.ds(pl.multiple_of(i * self.rows, 16), self.rows)
+
+    def plane(self, o):
+        p = lax.rem(self.me + o, self.peers)
+        return p, (p // self.nh, self.z, lax.rem(p, self.nh))
+
+    def scatter(self, o):
+        p, dev = self.plane(o)
+        return pltpu.make_async_remote_copy(
+            src_ref=self.out.at[self.slot(p)],
+            dst_ref=self.got.at[self.slot(self.me)],
+            send_sem=self.sems.at[0, 0, o],
+            recv_sem=self.sems.at[0, 1, o],
+            device_id=dev,
+            device_id_type=MESH,
+        )
+
+    def along(self, o):
+        q = lax.rem(self.z + o, self.nz)
+        return pltpu.make_async_remote_copy(
+            src_ref=self.deep.at[self.slot(self.z)],
+            dst_ref=self.deep.at[self.slot(self.z)],
+            send_sem=self.sems.at[1, 0, o],
+            recv_sem=self.sems.at[1, 1, o],
+            device_id=(self.b, q, self.h),
+            device_id_type=MESH,
+        )
+
+    def gather(self, o):
+        _, dev = self.plane(o)
+        return pltpu.make_async_remote_copy(
+            src_ref=self.full.at[self.slot(self.me)],
+            dst_ref=self.full.at[self.slot(self.me)],
+            send_sem=self.sems.at[2, 0, o],
+            recv_sem=self.sems.at[2, 1, o],
+            device_id=dev,
+            device_id_type=MESH,
+        )
+
+    def start(self):
+        pad = self.peers * self.rows - self.mats * 128
+        if pad:
+            self.out[pl.ds(self.mats * 128, pad)] = jnp.zeros((pad, 128), jnp.bfloat16)
+        for o in range(1, self.peers):
+            self.scatter(o).start()
+
+    def middle(self):
+        total = self.out[self.slot(self.me)].astype(jnp.float32)
+        for o in range(1, self.peers):
+            self.scatter(o).wait()
+            src = lax.rem(self.me - o + self.peers, self.peers)
+            total = total + self.got[self.slot(src)].astype(jnp.float32)
+        self.deep[self.slot(self.z)] = total.astype(jnp.bfloat16)
+        for o in range(1, self.nz):
+            self.along(o).start()
+
+    def last(self):
+        for o in range(1, self.nz):
+            self.along(o).wait()
+        total = self.deep[pl.ds(0, self.rows)].astype(jnp.float32)
+        for q in range(1, self.nz):
+            total = total + self.deep[pl.ds(q * self.rows, self.rows)].astype(jnp.float32)
+        self.full[self.slot(self.me)] = total.astype(jnp.bfloat16)
+        for o in range(1, self.peers):
+            self.gather(o).start()
+
+    def finish(self):
+        for o in range(1, self.peers):
+            self.gather(o).wait()
+
+
+def greet(dims):
+    nb, nz, nh = dims
+    b, z, h = (lax.axis_index(a) for a in AXES)
+    me = b * nh + h
+    barrier = pltpu.get_barrier_semaphore()
+    for o in range(1, nb * nh):
+        p = lax.rem(me + o, nb * nh)
+        pl.semaphore_signal(
+            barrier, inc=1, device_id=(p // nh, z, lax.rem(p, nh)), device_id_type=MESH
+        )
+    for o in range(1, nz):
+        pl.semaphore_signal(
+            barrier, inc=1, device_id=(b, lax.rem(z + o, nz), h), device_id_type=MESH
+        )
+    pl.semaphore_wait(barrier, nb * nh - 1 + nz - 1)
+
+
+def sum_kernel(dims, gs_ref, gt_ref, gd_ref, os_ref, ot_ref, od_ref, *refs):
+    greet(dims)
+    total = Sum(dims, 15, refs)
+    for i in range(15):
+        part = gs_ref[i // 3, i % 3] if i < 9 else gt_ref[i - 9] if i < 12 else gd_ref[i - 12]
+        total.out[pl.ds(i * 128, 128)] = part.astype(jnp.bfloat16)
+    total.start()
+    total.middle()
+    total.last()
+    total.finish()
+    for i in range(15):
+        part = total.full[pl.ds(i * 128, 128)].astype(jnp.float32)
+        if i < 9:
+            os_ref[i // 3, i % 3] = part
+        elif i < 12:
+            ot_ref[i - 9] = part
+        else:
+            od_ref[i - 12] = part
+
+
+def all_sum(gs, gt, gd):
+    dims = tuple(lax.axis_size(a) for a in AXES)
+    return pl.pallas_call(
+        functools.partial(sum_kernel, dims),
+        out_shape=[jax.ShapeDtypeStruct(g.shape, jnp.float32) for g in (gs, gt, gd)],
+        in_specs=[pl.BlockSpec(memory_space=pltpu.VMEM)] * 3,
+        out_specs=[pl.BlockSpec(memory_space=pltpu.VMEM)] * 3,
+        scratch_shapes=sum_scratch(15, dims[0] * dims[2], dims[1]),
+        compiler_params=pltpu.CompilerParams(
+            collective_id=0, has_side_effects=True, vmem_limit_bytes=24 * 1024 * 1024
+        ),
+    )(gs, gt, gd)
 
 
 def with_halo(block, sides, width):
@@ -122,9 +277,7 @@
     g_prepad = with_halo(g_pre, (("height", 2),), 1)
     flip_s = jnp.transpose(w_spatial[::-1, ::-1], (0, 1, 3, 2))
     grad_features = (g_resid + spatial(g_prepad, flip_s)).astype(jnp.bfloat16)
-    grad_spatial, grad_temporal, grad_down = lax.psum(
-        (grad_spatial, grad_temporal, grad_down), ("batch", "tm", "height")
-    )
+    grad_spatial, grad_temporal, grad_down = all_sum(grad_spatial, grad_temporal, grad_down)
     return (downsampled, grad_features, grad_spatial, grad_temporal, grad_down)
 
 

time: 203 us -> 78.9 us (0.39)
  waiting for transfers between devices: 131 us -> 4.11 us
  Pallas kernels: 0 us -> 26.1 us
  between operations: 14.6 us -> 1.18 us
  matrix products: 19.9 us -> 16.1 us
  local copies, waits for them, and re-layouts: 7.92 us -> 4.14 us
  other arithmetic: 2.63 us -> 0.58 us
    psum x1 -> x0, waiting for transfers between devices: 127 us -> none  [per_device(): lax.psum((grad_spatial, grad_temporal, grad_down), ('batch', 'tm', 'heigh...]
    pallas_call x0 -> x1, Pallas kernels: none -> 26.1 us  [all_sum(): pl.pallas_call(functools.partial(sum_kernel, dims), out_shape=[jax.ShapeD...]
    unnamed x33 -> x15, local copies, waits for them, and re-layouts: 6.83 us -> 3.07 us
  transfers between devices with their start and end apart: 11 -> 10, of which waited for: 2 -> 2; matrix products, arithmetic and copies ran while one was open for 11% -> 17% of each run, Pallas kernels for 0% -> 0%
where the time goes in v1:
time: 78.9 us; the launch traced here: 78.3 us
  starting transfers between devices  26.1 us (33%)
  Pallas kernels  26.1 us (33%)
  matrix products  16.1 us (20%)
  local copies, waits for them, and re-layouts  4.14 us (5%)
  waiting for transfers between devices  4.11 us (5%)
  between operations  1.18 us (1%)
    pallas_call x1, Pallas kernels, all_sum(): pl.pallas_call(functools.partial(sum_kernel, dims), out_shape=[jax.ShapeD...  26.1 us
    ppermute x4, starting transfers between devices, with_halo(): lax.ppermute(lax.slice_in_dim(block, block.shape[dim] - width, None, axis...  15.4 us
    dot_general x18, matrix products, spatial(): jnp.einsum('bfhwc,cd->bfhwd', wide[:, :, dy:dy + rows, dx:dx + cols], ker...  6.18 us
    ppermute x4, starting transfers between devices, with_halo(): lax.ppermute(lax.slice_in_dim(block, 0, width, axis=dim), axis, backward)  5.48 us
    ppermute x2, starting transfers between devices, from_behind(): return lax.ppermute(shard, axis, pairs)  5.22 us
    ppermute x4, waiting for transfers between devices, with_halo(): lax.ppermute(lax.slice_in_dim(block, 0, width, axis=dim), axis, backward)  4.09 us
    dot_general x9, matrix products, spatial_grad(): jnp.einsum('bfhwc,bfhwd->cd', wide[:, :, dy:dy + rows, dx:dx + cols], gra...  3.07 us
    unnamed x15, local copies, waits for them, and re-layouts  3.07 us
  transfers between devices with their start and end apart: 10, of which 2 were waited for; matrix products, arithmetic and copies ran while one was open for 17% of the time, Pallas kernels for 0%

profile of v1, /device:TPU:0, one launch (start us, length us, event | category | flops | bytes accessed | tf_op | source)
XLA Modules:
  0.0 78.3 jit_solution(8222974121217679016)
XLA Ops:
  0.7 0.9 %fusion.130 = (bf16[1,2,1,128,128]{4,3,2,1,0:T(8,128)(2,1)S(1)}, bf16[1,2,1,128,128]{4,3,2,1,0:T(8,128)(2,1)S(1)}) fusion(bf16[1,2,8,128,128]{4,3,2,1,0:T(8,128)(2,1)} %param.5), kind=kLoop, calls=%fused_computation.200 | loop fusion | bytes 262144 | tf_op jit(solution)/shard_map/slice | solution.py:168
  1.6 2.4 %collective-permute-start = (bf16[1,2,1,128,128]{4,3,2,1,0:T(8,128)(2,1)S(1)}, bf16[1,2,1,128,128]{4,3,2,1,0:T(8,128)(2,1)S(1)}, u32[]{:S(2)}, u32[]{:S(2)}) collective-permute-start(bf16[1,2,1,128,128]{4,3,2,1,0:T(8,128)(2,1)S(1)} %get-tuple-element.17), channel_id=1, source_target_pairs={{0,1},{1,2},{2,3},{4,5},{5,6},{6,7},{8,9},{9,10},{10,11},{12,13},{... | collective-permute-start | bytes 196616 | tf_op jit(solution)/shard_map/ppermute | solution.py:167
  4.0 1.4 %collective-permute-start.1 = (bf16[1,2,1,128,128]{4,3,2,1,0:T(8,128)(2,1)S(1)}, bf16[1,2,1,128,128]{4,3,2,1,0:T(8,128)(2,1)S(1)}, u32[]{:S(2)}, u32[]{:S(2)}) collective-permute-start(bf16[1,2,1,128,128]{4,3,2,1,0:T(8,128)(2,1)S(1)} %get-tuple-element.18), channel_id=1, source_target_pairs={{1,0},{2,1},{3,2},{5,4},{6,5},{7,6},{9,8},{10,9},{11,10},{13,12},{... | collective-permute-start | bytes 196616 | tf_op jit(solution)/shard_map/ppermute | solution.py:170
  5.4 1.3 %collective-permute-start.5 = (bf16[1,1,8,128,128]{4,3,2,1,0:T(8,128)(2,1)}, bf16[1,1,8,128,128]{4,3,2,1,0:T(8,128)(2,1)S(1)}, u32[]{:S(2)}, u32[]{:S(2)}) collective-permute-start(bf16[1,1,8,128,128]{4,3,2,1,0:T(8,128)(2,1)} %param.9), channel_id=1, source_target_pairs={{4,0},{8,4},{12,8},{5,1},{9,5},{13,9},{6,2},{10,6},{14,10},{7,3},{... | collective-permute-start | bytes 786440 | tf_op jit(solution)/shard_map/ppermute | solution.py:178
  6.7 1.2 %fusion.60 = f32[8,128,128]{2,1,0:T(8,128)S(1)} fusion(bf16[1,1,8,128,128]{4,3,2,1,0:T(8,128)(2,1)} %param.9, bf16[3,128,128]{2,1,0:T(8,128)(2,1)} %param.8), kind=kOutput, calls=%fused_computation.117 | convolution fusion | flops 33554432 | bytes 819200 | tf_op jit(solution)/shard_map/bfhwd,cd->bfhwc/dot_general | solution.py:256
  8.3 0.5 copy-done.2
  9.8 0.3 fusion.51
  10.1 0.3 convolution_add_fusion.15
  10.4 0.3 convolution_add_fusion.14
  11.3 0.3 convolution_add_fusion.11
  11.6 0.3 convolution_add_fusion.10
  11.9 0.5 multiply_convert_fusion
  12.4 1.3 %collective-permute-start.3 = (bf16[1,1,8,128,128]{4,3,2,1,0:T(8,128)(2,1)S(1)}, bf16[1,1,8,128,128]{4,3,2,1,0:T(8,128)(2,1)S(1)}, u32[]{:S(2)}, u32[]{:S(2)}) collective-permute-start(bf16[1,1,8,128,128]{4,3,2,1,0:T(8,128)(2,1)S(1)} %get-tuple-element.16), channel_id=1, source_target_pairs={{4,0},{8,4},{12,8},{5,1},{9,5},{13,9},{6,2},{10,6},{14,10},{7,3},{... | collective-permute-start | bytes 786440 | tf_op jit(solution)/shard_map/ppermute | solution.py:170
  13.7 5.4 %collective-permute-start.2 = (bf16[1,1,8,128,128]{4,3,2,1,0:T(8,128)(2,1)S(1)}, bf16[1,1,8,128,128]{4,3,2,1,0:T(8,128)(2,1)S(1)}, u32[]{:S(2)}, u32[]{:S(2)}) collective-permute-start(bf16[1,1,8,128,128]{4,3,2,1,0:T(8,128)(2,1)S(1)} %get-tuple-element.15), channel_id=1, source_target_pairs={{0,4},{4,8},{8,12},{1,5},{5,9},{9,13},{2,6},{6,10},{10,14},{3,7},{... | collective-permute-start | bytes 786440 | tf_op jit(solution)/shard_map/ppermute | solution.py:167
  19.8 0.3 fusion.75
  20.1 0.3 convolution_bitcast_fusion.1
  20.5 1.3 %collective-permute-start.7 = (bf16[1,1,8,128,128]{4,3,2,1,0:T(8,128)(2,1)S(1)}, bf16[1,1,8,128,128]{4,3,2,1,0:T(8,128)(2,1)S(1)}, u32[]{:S(2)}, u32[]{:S(2)}) collective-permute-start(bf16[1,1,8,128,128]{4,3,2,1,0:T(8,128)(2,1)S(1)} %get-tuple-element.14), channel_id=1, source_target_pairs={{4,0},{8,4},{12,8},{5,1},{9,5},{13,9},{6,2},{10,6},{14,10},{7,3},{... | collective-permute-start | bytes 786440 | tf_op jit(solution)/shard_map/ppermute | solution.py:170
  21.8 4.6 %collective-permute-start.6 = (bf16[1,1,8,128,128]{4,3,2,1,0:T(8,128)(2,1)S(1)}, bf16[1,1,8,128,128]{4,3,2,1,0:T(8,128)(2,1)S(1)}, u32[]{:S(2)}, u32[]{:S(2)}) collective-permute-start(bf16[1,1,8,128,128]{4,3,2,1,0:T(8,128)(2,1)S(1)} %get-tuple-element.13), channel_id=1, source_target_pairs={{0,4},{4,8},{8,12},{1,5},{5,9},{9,13},{2,6},{6,10},{10,14},{3,7},{... | collective-permute-start | bytes 786440 | tf_op jit(solution)/shard_map/ppermute | solution.py:167
  26.3 0.3 fusion.73
  26.6 0.3 fusion.11
  27.0 0.3 convolution_bitcast_fusion.12
  27.7 3.9 %collective-permute-start.4 = (bf16[1,1,8,128,128]{4,3,2,1,0:T(8,128)(2,1)S(1)}, bf16[1,1,8,128,128]{4,3,2,1,0:T(8,128)(2,1)S(1)}, u32[]{:S(2)}, u32[]{:S(2)}) collective-permute-start(bf16[1,1,8,128,128]{4,3,2,1,0:T(8,128)(2,1)S(1)} %slice.271), channel_id=1, source_target_pairs={{0,4},{4,8},{8,12},{1,5},{5,9},{9,13},{2,6},{6,10},{10,14},{3,7},{... | collective-permute-start | bytes 786440 | tf_op jit(solution)/shard_map/ppermute | solution.py:178
  31.7 0.3 convolution_bitcast_fusion
  32.0 0.4 convolution_bitcast_fusion.2
  33.0 0.6 fusion.10
  33.6 0.3 fusion.25
  33.9 0.3 fusion.24
  34.2 0.3 fusion.23
  34.6 0.3 fusion.22
  34.9 0.3 fusion.21
  35.3 0.3 fusion.20
  35.6 0.3 fusion.19
  36.0 3.0 %collective-permute-start.8 = (bf16[1,2,1,128,128]{4,3,2,1,0:T(8,128)(2,1)S(1)}, bf16[1,2,1,128,128]{4,3,2,1,0:T(8,128)(2,1)S(1)}, u32[]{:S(2)}, u32[]{:S(2)}) collective-permute-start(bf16[1,2,1,128,128]{4,3,2,1,0:T(8,128)(2,1)S(1)} %get-tuple-element.11), channel_id=1, source_target_pairs={{0,1},{1,2},{2,3},{4,5},{5,6},{6,7},{8,9},{9,10},{10,11},{12,13},{... | collective-permute-start | bytes 196616 | tf_op jit(solution)/shard_map/ppermute | solution.py:167
  39.1 1.5 %collective-permute-start.9 = (bf16[1,2,1,128,128]{4,3,2,1,0:T(8,128)(2,1)S(1)}, bf16[1,2,1,128,128]{4,3,2,1,0:T(8,128)(2,1)S(1)}, u32[]{:S(2)}, u32[]{:S(2)}) collective-permute-start(bf16[1,2,1,128,128]{4,3,2,1,0:T(8,128)(2,1)S(1)} %get-tuple-element.12), channel_id=1, source_target_pairs={{1,0},{2,1},{3,2},{5,4},{6,5},{7,6},{9,8},{10,9},{11,10},{13,12},{... | collective-permute-start | bytes 196616 | tf_op jit(solution)/shard_map/ppermute | solution.py:170
  40.5 0.3 fusion.18
  40.9 0.3 fusion.17
  41.2 3.9 %collective-permute-done.9 = bf16[1,2,1,128,128]{4,3,2,1,0:T(8,128)(2,1)S(1)} collective-permute-done((bf16[1,2,1,128,128]{4,3,2,1,0:T(8,128)(2,1)S(1)}, bf16[1,2,1,128,128]{4,3,2,1,0:T(8,128)(2,1)S(1)}, u32[]{:S(2)}, u32[]{:S(2)}) %collective-permute-start.9) | collective-permute-done | bytes 65568 | tf_op jit(solution)/shard_map/ppermute | solution.py:170
  45.6 0.3 fusion.29
  46.2 26.1 %shard_map.92 = (f32[3,3,128,128]{3,2,1,0:T(8,128)S(1)}, f32[3,128,128]{2,1,0:T(8,128)S(1)}, f32[3,128,128]{2,1,0:T(8,128)S(1)}) custom-call(f32[3,3,128,128]{3,2,1,0:T(8,128)S(1)} %bitcast.431, f32[3,128,128]{2,1,0:T(8,128)S(1)} %pad_maximum_fusion.10.gt_ref, f32[3,128,128]{2,1,0:T(8,128)S(1)} %pad_maximum_fusion.11.gd_ref), custom_call_target="tpu_custom_call" | custom-call | tf_op jit(solution)/shard_map/pallas_call | solution.py:150
  72.3 0.3 convolution_add_fusion.6
  72.6 0.3 convolution_add_fusion.5
  72.9 0.3 convolution_add_fusion.4
  73.5 0.3 convolution_add_fusion.2
  74.1 1.2 %fusion.13 = bf16[1,2,8,128,128]{4,3,2,1,0:T(8,128)(2,1)} fusion(f32[2,8,128,128]{3,2,1,0:T(8,128)S(1)} %fusion.29, f32[2,8,128,128]{3,2,1,0:T(8,128)S(1)} %convolution_add_fusion.1, f32[1,1,1,8,128,128]{5,4,3,2,1,0:T(8,128)S(1)} %bitcast.444, f32[1,1,1,8,128,128]{5,4,3,2,1,0:T(8,128)S(1)} %bitcast.442, ...), kind=kOutput, calls=%fused_computation.31 | convolution fusion | flops 68681728 | bytes 4292608 | tf_op jit(solution)/shard_map/bfhwc,cd->bfhwd/dot_general | solution.py:188
  75.2 0.9 %fusion.16 = bf16[1,1,8,128,128]{4,3,2,1,0:T(8,128)(2,1)} fusion(f32[8,128,128]{2,1,0:T(8,128)S(1)} %fusion.65, f32[8,128,128]{2,1,0:T(8,128)S(1)} %fusion.69, bf16[1,1,8,128,128]{4,3,2,1,0:T(8,128)(2,1)S(1)} %collective-permute-done.4, bf16[3,128,128]{2,1,0:T(8,128)(2,1)S(1)} %copy-done.4), kind=kOutput, calls=%fused_computation.36 | convolution fusion | flops 33947648 | bytes 1605632 | tf_op jit(solution)/shard_map/bfhwc,cd->bfhwd/dot_general | solution.py:245
  76.1 0.8 %copy.91 = f32[3,3,128,128]{3,2,1,0:T(8,128)} copy(f32[3,3,128,128]{3,2,1,0:T(8,128)S(1)} %get-tuple-element.28) | data formatting | bytes 1179648
  77.0 0.7 copy.92
  77.6 0.7 copy.93
  (47 shorter events, 4.9 us)
Async XLA Ops:
  0.6 7.3 %copy-start.1 = (bf16[1,1,8,128,128]{4,3,2,1,0:T(8,128)(2,1)S(1)}, bf16[1,1,8,128,128]{4,3,2,1,0:T(8,128)(2,1)}, u32[]{:S(2)}) copy-start(bf16[1,1,8,128,128]{4,3,2,1,0:T(8,128)(2,1)} %param.9) | copy-start | bytes 786436
  0.6 7.3 %copy-start.4 = (bf16[3,128,128]{2,1,0:T(8,128)(2,1)S(1)}, bf16[3,128,128]{2,1,0:T(8,128)(2,1)}, u32[]{:S(2)}) copy-start(bf16[3,128,128]{2,1,0:T(8,128)(2,1)} %param.8) | copy-start | bytes 294916
  1.6 7.5 %collective-permute-start = (bf16[1,2,1,128,128]{4,3,2,1,0:T(8,128)(2,1)S(1)}, bf16[1,2,1,128,128]{4,3,2,1,0:T(8,128)(2,1)S(1)}, u32[]{:S(2)}, u32[]{:S(2)}) collective-permute-start(bf16[1,2,1,128,128]{4,3,2,1,0:T(8,128)(2,1)S(1)} %get-tuple-element.17), channel_id=1, source_target_pairs={{0,1},{1,2},{2,3},{4,5},{5,6},{6,7},{8,9},{9,10},{10,11},{12,13},{... | collective-permute-start | bytes 196616 | tf_op jit(solution)/shard_map/ppermute | solution.py:167
  4.0 4.2 %copy-start.3 = (bf16[3,128,128]{2,1,0:T(8,128)(2,1)S(1)}, bf16[3,128,128]{2,1,0:T(8,128)(2,1)}, u32[]{:S(2)}) copy-start(bf16[3,128,128]{2,1,0:T(8,128)(2,1)} %param.7) | copy-start | bytes 294916
  4.0 5.4 %collective-permute-start.1 = (bf16[1,2,1,128,128]{4,3,2,1,0:T(8,128)(2,1)S(1)}, bf16[1,2,1,128,128]{4,3,2,1,0:T(8,128)(2,1)S(1)}, u32[]{:S(2)}, u32[]{:S(2)}) collective-permute-start(bf16[1,2,1,128,128]{4,3,2,1,0:T(8,128)(2,1)S(1)} %get-tuple-element.18), channel_id=1, source_target_pairs={{1,0},{2,1},{3,2},{5,4},{6,5},{7,6},{9,8},{10,9},{11,10},{13,12},{... | collective-permute-start | bytes 196616 | tf_op jit(solution)/shard_map/ppermute | solution.py:170
  5.4 14.0 %collective-permute-start.5 = (bf16[1,1,8,128,128]{4,3,2,1,0:T(8,128)(2,1)}, bf16[1,1,8,128,128]{4,3,2,1,0:T(8,128)(2,1)S(1)}, u32[]{:S(2)}, u32[]{:S(2)}) collective-permute-start(bf16[1,1,8,128,128]{4,3,2,1,0:T(8,128)(2,1)} %param.9), channel_id=1, source_target_pairs={{4,0},{8,4},{12,8},{5,1},{9,5},{13,9},{6,2},{10,6},{14,10},{7,3},{... | collective-permute-start | bytes 786440 | tf_op jit(solution)/shard_map/ppermute | solution.py:178
  7.9 1.0 %copy-start.2 = (bf16[3,3,128,128]{3,2,1,0:T(8,128)(2,1)S(1)}, bf16[3,3,128,128]{3,2,1,0:T(8,128)(2,1)}, u32[]{:S(2)}) copy-start(bf16[3,3,128,128]{3,2,1,0:T(8,128)(2,1)} %param.6) | copy-start | bytes 884740
  8.1 1.2 %copy-start = (bf16[1,2,8,128,128]{4,3,2,1,0:T(8,128)(2,1)S(1)}, bf16[1,2,8,128,128]{4,3,2,1,0:T(8,128)(2,1)}, u32[]{:S(2)}) copy-start(bf16[1,2,8,128,128]{4,3,2,1,0:T(8,128)(2,1)} %param.5) | copy-start | bytes 1572868
  12.4 13.9 %collective-permute-start.3 = (bf16[1,1,8,128,128]{4,3,2,1,0:T(8,128)(2,1)S(1)}, bf16[1,1,8,128,128]{4,3,2,1,0:T(8,128)(2,1)S(1)}, u32[]{:S(2)}, u32[]{:S(2)}) collective-permute-start(bf16[1,1,8,128,128]{4,3,2,1,0:T(8,128)(2,1)S(1)} %get-tuple-element.16), channel_id=1, source_target_pairs={{4,0},{8,4},{12,8},{5,1},{9,5},{13,9},{6,2},{10,6},{14,10},{7,3},{... | collective-permute-start | bytes 786440 | tf_op jit(solution)/shard_map/ppermute | solution.py:170
  13.7 12.9 %collective-permute-start.2 = (bf16[1,1,8,128,128]{4,3,2,1,0:T(8,128)(2,1)S(1)}, bf16[1,1,8,128,128]{4,3,2,1,0:T(8,128)(2,1)S(1)}, u32[]{:S(2)}, u32[]{:S(2)}) collective-permute-start(bf16[1,1,8,128,128]{4,3,2,1,0:T(8,128)(2,1)S(1)} %get-tuple-element.15), channel_id=1, source_target_pairs={{0,4},{4,8},{8,12},{1,5},{5,9},{9,13},{2,6},{6,10},{10,14},{3,7},{... | collective-permute-start | bytes 786440 | tf_op jit(solution)/shard_map/ppermute | solution.py:167
  20.5 12.2 %collective-permute-start.7 = (bf16[1,1,8,128,128]{4,3,2,1,0:T(8,128)(2,1)S(1)}, bf16[1,1,8,128,128]{4,3,2,1,0:T(8,128)(2,1)S(1)}, u32[]{:S(2)}, u32[]{:S(2)}) collective-permute-start(bf16[1,1,8,128,128]{4,3,2,1,0:T(8,128)(2,1)S(1)} %get-tuple-element.14), channel_id=1, source_target_pairs={{4,0},{8,4},{12,8},{5,1},{9,5},{13,9},{6,2},{10,6},{14,10},{7,3},{... | collective-permute-start | bytes 786440 | tf_op jit(solution)/shard_map/ppermute | solution.py:170
  21.8 11.2 %collective-permute-start.6 = (bf16[1,1,8,128,128]{4,3,2,1,0:T(8,128)(2,1)S(1)}, bf16[1,1,8,128,128]{4,3,2,1,0:T(8,128)(2,1)S(1)}, u32[]{:S(2)}, u32[]{:S(2)}) collective-permute-start(bf16[1,1,8,128,128]{4,3,2,1,0:T(8,128)(2,1)S(1)} %get-tuple-element.13), channel_id=1, source_target_pairs={{0,4},{4,8},{8,12},{1,5},{5,9},{9,13},{2,6},{6,10},{10,14},{3,7},{... | collective-permute-start | bytes 786440 | tf_op jit(solution)/shard_map/ppermute | solution.py:167
  27.7 18.2 %collective-permute-start.4 = (bf16[1,1,8,128,128]{4,3,2,1,0:T(8,128)(2,1)S(1)}, bf16[1,1,8,128,128]{4,3,2,1,0:T(8,128)(2,1)S(1)}, u32[]{:S(2)}, u32[]{:S(2)}) collective-permute-start(bf16[1,1,8,128,128]{4,3,2,1,0:T(8,128)(2,1)S(1)} %slice.271), channel_id=1, source_target_pairs={{0,4},{4,8},{8,12},{1,5},{5,9},{9,13},{2,6},{6,10},{10,14},{3,7},{... | collective-permute-start | bytes 786440 | tf_op jit(solution)/shard_map/ppermute | solution.py:178
  36.0 5.2 %collective-permute-start.8 = (bf16[1,2,1,128,128]{4,3,2,1,0:T(8,128)(2,1)S(1)}, bf16[1,2,1,128,128]{4,3,2,1,0:T(8,128)(2,1)S(1)}, u32[]{:S(2)}, u32[]{:S(2)}) collective-permute-start(bf16[1,2,1,128,128]{4,3,2,1,0:T(8,128)(2,1)S(1)} %get-tuple-element.11), channel_id=1, source_target_pairs={{0,1},{1,2},{2,3},{4,5},{5,6},{6,7},{8,9},{9,10},{10,11},{12,13},{... | collective-permute-start | bytes 196616 | tf_op jit(solution)/shard_map/ppermute | solution.py:167
  39.1 6.1 %collective-permute-start.9 = (bf16[1,2,1,128,128]{4,3,2,1,0:T(8,128)(2,1)S(1)}, bf16[1,2,1,128,128]{4,3,2,1,0:T(8,128)(2,1)S(1)}, u32[]{:S(2)}, u32[]{:S(2)}) collective-permute-start(bf16[1,2,1,128,128]{4,3,2,1,0:T(8,128)(2,1)S(1)} %get-tuple-element.12), channel_id=1, source_target_pairs={{1,0},{2,1},{3,2},{5,4},{6,5},{7,6},{9,8},{10,9},{11,10},{13,12},{... | collective-permute-start | bytes 196616 | tf_op jit(solution)/shard_map/ppermute | solution.py:170

commit v2 on v1

v2 whole, which is shorter than its diff:
```python
import functools

import jax
import jax.numpy as jnp
from jax import lax
from jax.experimental import pallas as pl
from jax.experimental.pallas import tpu as pltpu
from jax.sharding import PartitionSpec as P

MESH = pl.DeviceIdType.MESH
AXES = ("batch", "tm", "height")


def rows_each(mats, peers):
    return 16 * pl.cdiv(mats * 128, 16 * peers)


def sum_scratch(mats, peers, depth):
    rows = rows_each(mats, peers)
    return [
        pltpu.VMEM((peers * rows, 128), jnp.bfloat16),
        pltpu.VMEM((peers * rows, 128), jnp.bfloat16),
        pltpu.VMEM((depth * rows, 128), jnp.bfloat16),
        pltpu.VMEM((peers * rows, 128), jnp.bfloat16),
        pltpu.SemaphoreType.DMA((3, 2, max(peers, depth))),
    ]


class Sum:
    def __init__(self, dims, mats, refs):
        self.nb, self.nz, self.nh = dims
        self.mats = mats
        self.peers = self.nb * self.nh
        self.rows = rows_each(mats, self.peers)
        self.out, self.got, self.deep, self.full, self.sems = refs
        self.b, self.z, self.h = (lax.axis_index(a) for a in AXES)
        self.me = self.b * self.nh + self.h

    def slot(self, i):
        return pl.ds(pl.multiple_of(i * self.rows, 16), self.rows)

    def plane(self, o):
        p = lax.rem(self.me + o, self.peers)
        return p, (p // self.nh, self.z, lax.rem(p, self.nh))

    def scatter(self, o):
        p, dev = self.plane(o)
        return pltpu.make_async_remote_copy(
            src_ref=self.out.at[self.slot(p)],
            dst_ref=self.got.at[self.slot(self.me)],
            send_sem=self.sems.at[0, 0, o],
            recv_sem=self.sems.at[0, 1, o],
            device_id=dev,
            device_id_type=MESH,
        )

    def along(self, o):
        q = lax.rem(self.z + o, self.nz)
        return pltpu.make_async_remote_copy(
            src_ref=self.deep.at[self.slot(self.z)],
            dst_ref=self.deep.at[self.slot(self.z)],
            send_sem=self.sems.at[1, 0, o],
            recv_sem=self.sems.at[1, 1, o],
            device_id=(self.b, q, self.h),
            device_id_type=MESH,
        )

    def gather(self, o):
        _, dev = self.plane(o)
        return pltpu.make_async_remote_copy(
            src_ref=self.full.at[self.slot(self.me)],
            dst_ref=self.full.at[self.slot(self.me)],
            send_sem=self.sems.at[2, 0, o],
            recv_sem=self.sems.at[2, 1, o],
            device_id=dev,
            device_id_type=MESH,
        )

    def start(self):
        pad = self.peers * self.rows - self.mats * 128
        if pad:
            self.out[pl.ds(self.mats * 128, pad)] = jnp.zeros((pad, 128), jnp.bfloat16)
        for o in range(1, self.peers):
            self.scatter(o).start()

    def middle(self):
        total = self.out[self.slot(self.me)].astype(jnp.float32)
        for o in range(1, self.peers):
            self.scatter(o).wait()
            src = lax.rem(self.me - o + self.peers, self.peers)
            total = total + self.got[self.slot(src)].astype(jnp.float32)
        self.deep[self.slot(self.z)] = total.astype(jnp.bfloat16)
        for o in range(1, self.nz):
            self.along(o).start()

    def last(self):
        for o in range(1, self.nz):
            self.along(o).wait()
        total = self.deep[pl.ds(0, self.rows)].astype(jnp.float32)
        for q in range(1, self.nz):
            total = total + self.deep[pl.ds(q * self.rows, self.rows)].astype(jnp.float32)
        self.full[self.slot(self.me)] = total.astype(jnp.bfloat16)
        for o in range(1, self.peers):
            self.gather(o).start()

    def finish(self):
        for o in range(1, self.peers):
            self.gather(o).wait()


def greet(dims):
    nb, nz, nh = dims
    b, z, h = (lax.axis_index(a) for a in AXES)
    me = b * nh + h
    barrier = pltpu.get_barrier_semaphore()
    for o in range(1, nb * nh):
        p = lax.rem(me + o, nb * nh)
        pl.semaphore_signal(
            barrier, inc=1, device_id=(p // nh, z, lax.rem(p, nh)), device_id_type=MESH
        )
    for o in range(1, nz):
        pl.semaphore_signal(
            barrier, inc=1, device_id=(b, lax.rem(z + o, nz), h), device_id_type=MESH
        )
    pl.semaphore_wait(barrier, nb * nh - 1 + nz - 1)


class Edge:
    def __init__(self, src, dst, sems, axis, step):
        size, at = lax.axis_size(axis), lax.axis_index(axis)
        self.sends = at < size - 1 if step > 0 else at > 0
        self.gets = at > 0 if step > 0 else at < size - 1
        self.copy = pltpu.make_async_remote_copy(
            src_ref=src,
            dst_ref=dst,
            send_sem=sems.at[0],
            recv_sem=sems.at[1],
            device_id=tuple(lax.axis_index(a) + (step if a == axis else 0) for a in AXES),
            device_id_type=MESH,
        )
        self.dst = dst

    def start(self):
        @pl.when(self.sends)
        def _():
            self.copy.start()

        @pl.when(jnp.logical_not(self.gets))
        def _():
            self.dst[...] = jnp.zeros(self.dst.shape, self.dst.dtype)

    def arrive(self):
        @pl.when(self.gets)
        def _():
            self.copy.wait_recv()

    def leave(self):
        @pl.when(self.sends)
        def _():
            self.copy.wait_send()


def dot(a, b):
    return jnp.dot(a, b, preferred_element_type=jnp.float32)


def from_left(v, col):
    return jnp.where(col == 0, 0.0, pltpu.roll(v, 1, 0))


def from_right(v, col, width):
    return jnp.where(col == width - 1, 0.0, pltpu.roll(v, v.shape[0] - 1, 0))


def kernel(
    dims, step, x_ref, ws_ref, wt_ref, wd_ref, c_ref,
    down_ref, gx_ref, os_ref, ot_ref, od_ref,
    xp, xt, gp, gcat, act, slope, gres, gb, cm, cp, lcat, part, d_out, e_out, d_in, e_in,
    wf, wb, tcat, tflip, dflip, dback, edge_sems, *sums,
):
    _, rows, width, ch = x_ref.shape[1:]
    tokens = rows * width
    per = step * width
    half = len(sums) // 2
    big, small = Sum(dims, 9, sums[:half]), Sum(dims, 6, sums[half:])
    edges = [
        Edge(x_ref.at[0, :, rows - 1], xp.at[:, 0], edge_sems.at[0], "height", 1),
        Edge(x_ref.at[0, :, 0], xp.at[:, rows + 1], edge_sems.at[1], "height", -1),
        Edge(c_ref.at[0, 0], cm, edge_sems.at[2], "tm", 1),
        Edge(c_ref.at[0, 0], cp, edge_sems.at[3], "tm", -1),
        Edge(gp.at[:, rows], gp.at[:, 0], edge_sems.at[4], "height", 1),
        Edge(gp.at[:, 1], gp.at[:, rows + 1], edge_sems.at[5], "height", -1),
        Edge(d_out, d_in, edge_sems.at[6], "tm", 1),
        Edge(e_out, e_in, edge_sems.at[7], "tm", -1),
    ]
    inner = (lax.axis_index("tm") > 0).astype(jnp.float32)
    col = lax.broadcasted_iota(jnp.int32, (step, width, ch), 1).reshape(per, ch)

    greet(dims)
    for e in edges[:4]:
        e.start()
    for f in range(2):
        xp[f, pl.ds(1, rows)] = x_ref[0, f]
    for k in range(3):
        tcat[:, (2 - k) * ch : (3 - k) * ch] = wt_ref[k]
        tflip[k * ch : (k + 1) * ch, :] = wt_ref[k].T
        dflip[:, k * ch : (k + 1) * ch] = wd_ref[k].T
        for dx in range(3):
            w = ws_ref[k, dx]
            wf[k * ch : (k + 1) * ch, dx * ch : (dx + 1) * ch] = w
            wb[(2 - k) * ch : (3 - k) * ch, (2 - dx) * ch : (3 - dx) * ch] = w.T
    dback[0:ch, :] = dflip[:, 2 * ch : 3 * ch]
    dback[ch : 2 * ch, :] = dflip[:, 0:ch]

    def flat(v):
        return v.reshape(per, ch)

    def tall(v):
        return v.reshape(step, width, ch)

    def conv(ref, f, y, weights):
        wide = jnp.concatenate([flat(ref[f, pl.ds(y + dy, step)]) for dy in range(3)], axis=1)
        out = dot(wide, weights[...])
        return (
            out[:, ch : 2 * ch]
            + from_left(out[:, :ch], col)
            + from_right(out[:, 2 * ch :], col, width)
        )

    for e in edges[:2]:
        e.arrive()
    cuts = rows // step

    def forward(i, carry):
        f, y = i // cuts, (i % cuts) * step
        pre = conv(xp, f, y, wf)
        sig = jax.nn.sigmoid(pre)
        act[f, pl.ds(y, step)] = tall((pre * sig).astype(jnp.bfloat16))
        slope[f, pl.ds(y, step)] = tall(sig * (1.0 + pre * (1.0 - sig)))
        return carry

    lax.fori_loop(0, 2 * cuts, forward, 0)

    for f in range(2):
        xt[f] = xp[f].reshape((rows + 2) * width, ch).T

    for e in edges[2:4]:
        e.arrive()

    def backward(i, carry):
        at = pl.ds(i * step, step)
        c0, before, after = flat(c_ref[0, 0, at]), flat(cm[at]), flat(cp[at])
        g0 = dot(jnp.concatenate([before, c0], axis=1), dback[...]) * inner
        mid = dot(c0, dflip[:, ch:])
        far = dot(after, dflip[:, : 2 * ch])
        g1, g2, g3 = mid[:, :ch], mid[:, ch:] + far[:, :ch], far[:, ch:]
        gres[0, at] = tall(g1)
        gres[1, at] = tall(g2)
        g = [v.astype(jnp.bfloat16) for v in (g0, g1, g2, g3)]
        for n in range(4):
            gb[n, at] = tall(g[n])
        for a in range(2):
            wide = jnp.concatenate([g[a + 2], g[a + 1], g[a]], axis=1)
            gpre = dot(wide, tflip[...]) * flat(slope[a, at])
            low = gpre.astype(jnp.bfloat16)
            gp[a, pl.ds(i * step + 1, step)] = tall(low)
            gcat[a, at, :, :ch] = tall(from_right(gpre, col, width).astype(jnp.bfloat16))
            gcat[a, at, :, ch : 2 * ch] = tall(low)
            gcat[a, at, :, 2 * ch :] = tall(from_left(gpre, col).astype(jnp.bfloat16))
        return carry

    lax.fori_loop(0, cuts, backward, 0)
    for e in edges[4:6]:
        e.start()

    total = jnp.zeros((3 * ch, 3 * ch), jnp.float32)
    for f in range(2):
        left = jnp.concatenate(
            [xt[f, :, dy * width : dy * width + tokens] for dy in range(3)], axis=0
        )
        total = total + dot(left, gcat[f].reshape(tokens, 3 * ch))
    for dy in range(3):
        for dx in range(3):
            big.out[pl.ds((dy * 3 + dx) * ch, ch)] = total[
                dy * ch : (dy + 1) * ch, dx * ch : (dx + 1) * ch
            ].astype(jnp.bfloat16)
    big.start()

    def mixing(i, carry):
        at = pl.ds(i * step, step)
        y0 = dot(flat(act[0, at]), tcat[...])
        y1 = dot(flat(act[1, at]), tcat[...])
        x0 = flat(x_ref[0, 0, at]).astype(jnp.float32)
        x1 = flat(x_ref[0, 1, at]).astype(jnp.float32)
        l0 = (y0[:, :ch] * inner).astype(jnp.bfloat16)
        l1 = (x0 + y0[:, ch : 2 * ch] + y1[:, :ch]).astype(jnp.bfloat16)
        l2 = (x1 + y0[:, 2 * ch :] + y1[:, ch : 2 * ch]).astype(jnp.bfloat16)
        u = y1[:, 2 * ch :].astype(jnp.bfloat16)
        for n, v in enumerate((l0, l1, l2, u)):
            lcat[n, at] = tall(v)
        own = jnp.concatenate([l0, l1, l2], axis=1)
        part[at] = tall(dot(own, wd_ref[...].reshape(3 * ch, ch)))
        ahead = jnp.concatenate([l2, u], axis=1)
        d_out[at] = tall(dot(ahead, wd_ref[0:2].reshape(2 * ch, ch)).astype(jnp.bfloat16))
        e_out[at] = tall(dot(l0, wd_ref[2]).astype(jnp.bfloat16))
        return carry

    lax.fori_loop(0, cuts, mixing, 0)
    for e in edges[6:]:
        e.start()

    times = jnp.zeros((ch, 3 * ch), jnp.float32)
    for a in range(2):
        wide = jnp.concatenate([gb[n].reshape(tokens, ch) for n in (a + 2, a + 1, a)], axis=1)
        times = times + dot(act[a].reshape(tokens, ch).T, wide)
    left = jnp.concatenate([lcat[n].reshape(tokens, ch).T for n in range(4)], axis=0)
    wide = jnp.concatenate([v.reshape(tokens, ch) for v in (cp[...], c_ref[0, 0], cm[...])], axis=1)
    outer = dot(left, wide)

    def block(n, m):
        return outer[n * ch : (n + 1) * ch, m * ch : (m + 1) * ch]

    downs = (block(2, 0) + block(0, 1), block(1, 1) + block(3, 0), block(2, 1) + block(0, 2))
    for k in range(3):
        small.out[pl.ds(k * ch, ch)] = times[:, k * ch : (k + 1) * ch].astype(jnp.bfloat16)
        small.out[pl.ds((3 + k) * ch, ch)] = downs[k].astype(jnp.bfloat16)
    small.start()

    big.middle()
    for e in edges[4:6]:
        e.arrive()

    def features(f):
        def body(i, carry):
            at = pl.ds(i * step, step)
            out = conv(gp, f, i * step, wb) + flat(gres[f, at])
            gx_ref[0, f, at] = tall(out.astype(jnp.bfloat16))
            return carry

        lax.fori_loop(0, cuts, body, 0)

    features(0)
    small.middle()
    big.last()
    features(1)
    small.last()
    for e in edges[6:]:
        e.arrive()
    down_ref[0, 0] = (
        part[...] + d_in[...].astype(jnp.float32) + e_in[...].astype(jnp.float32)
    ).astype(jnp.bfloat16)
    big.finish()
    for i in range(9):
        os_ref[i // 3, i % 3] = big.full[pl.ds(i * ch, ch)].astype(jnp.float32)
    small.finish()
    for i in range(3):
        ot_ref[i] = small.full[pl.ds(i * ch, ch)].astype(jnp.float32)
        od_ref[i] = small.full[pl.ds((3 + i) * ch, ch)].astype(jnp.float32)
    for e in edges:
        e.leave()


def per_device(features, w_spatial, w_temporal, w_down, cotangent):
    dims = tuple(lax.axis_size(a) for a in AXES)
    _, frames, rows, width, ch = features.shape
    peers = dims[0] * dims[2]
    step = 4
    bf, f32 = jnp.bfloat16, jnp.float32
    frame = (rows, width, ch)
    return pl.pallas_call(
        functools.partial(kernel, dims, step),
        out_shape=[
            jax.ShapeDtypeStruct(cotangent.shape, bf),
            jax.ShapeDtypeStruct(features.shape, bf),
            jax.ShapeDtypeStruct(w_spatial.shape, f32),
            jax.ShapeDtypeStruct(w_temporal.shape, f32),
            jax.ShapeDtypeStruct(w_down.shape, f32),
        ],
        in_specs=[pl.BlockSpec(memory_space=pltpu.VMEM)] * 5,
        out_specs=[pl.BlockSpec(memory_space=pltpu.VMEM)] * 5,
        scratch_shapes=[
            pltpu.VMEM((2, rows + 2, width, ch), bf),
            pltpu.VMEM((2, ch, (rows + 2) * width), bf),
            pltpu.VMEM((2, rows + 2, width, ch), bf),
            pltpu.VMEM((2, rows, width, 3 * ch), bf),
            pltpu.VMEM((2,) + frame, bf),
            pltpu.VMEM((2,) + frame, f32),
            pltpu.VMEM((2,) + frame, f32),
            pltpu.VMEM((4,) + frame, bf),
            pltpu.VMEM(frame, bf),
            pltpu.VMEM(frame, bf),
            pltpu.VMEM((4,) + frame, bf),
            pltpu.VMEM(frame, f32),
            pltpu.VMEM(frame, bf),
            pltpu.VMEM(frame, bf),
            pltpu.VMEM(frame, bf),
            pltpu.VMEM(frame, bf),
            pltpu.VMEM((3 * ch, 3 * ch), bf),
            pltpu.VMEM((3 * ch, 3 * ch), bf),
            pltpu.VMEM((ch, 3 * ch), bf),
            pltpu.VMEM((3 * ch, ch), bf),
            pltpu.VMEM((ch, 3 * ch), bf),
            pltpu.VMEM((2 * ch, ch), bf),
            pltpu.SemaphoreType.DMA((8, 2)),
        ]
        + sum_scratch(9, peers, dims[1])
        + sum_scratch(6, peers, dims[1]),
        compiler_params=pltpu.CompilerParams(
            collective_id=0, has_side_effects=True, vmem_limit_bytes=40 * 1024 * 1024
        ),
    )(features, w_spatial, w_temporal, w_down, cotangent)


def solution(mesh):
    placed = (
        P("batch", "tm", "height", None, None),
        P(),
        P(),
        P(),
        P("batch", "tm", "height", None, None),
    )
    return jax.shard_map(
        per_device,
        mesh=mesh,
        in_specs=placed,
        out_specs=(
            P("batch", "tm", "height", None, None),
            P("batch", "tm", "height", None, None),
            P(),
            P(),
            P(),
        ),
        check_vma=False,
    )
```

time: 78.9 us -> 43.8 us (0.56)
  starting transfers between devices: 26.1 us -> 0 us
  matrix products: 16.1 us -> 0 us
  Pallas kernels: 26.1 us -> 34.4 us
  local copies, waits for them, and re-layouts: 4.14 us -> 8.39 us
  waiting for transfers between devices: 4.11 us -> 0 us
    ppermute x10 -> x0, starting transfers between devices: 26.1 us -> none  [the longest x4 15.4 us: with_halo(): lax.ppermute(lax.slice_in_dim(block, block.shape[dim] - width, None, axis...]
    dot_general x45 -> x0, matrix products: 16.1 us -> none  [the longest x18 6.18 us: spatial(): jnp.einsum('bfhwc,cd->bfhwd', wide[:, :, dy:dy + rows, dx:dx + cols], ker...]
    pallas_call x1, Pallas kernels: 26.1 us -> 34.4 us  [per_device(): pl.pallas_call(functools.partial(kernel, dims, step), out_shape=[jax.Shap...]
    unnamed x15, local copies, waits for them, and re-layouts: 3.07 us -> 8.39 us
    ppermute x10 -> x0, waiting for transfers between devices: 4.11 us -> none  [the longest x4 4.09 us: with_halo(): lax.ppermute(lax.slice_in_dim(block, 0, width, axis=dim), axis, backward)]
    slice x5 -> x0, local copies, waits for them, and re-layouts: 1.04 us -> none  [the longest x4 1.02 us: with_halo(): lax.slice_in_dim(block, block.shape[dim] - width, None, axis=dim)]
  transfers between devices with their start and end apart: 10 -> 0, of which waited for: 2 -> 0; matrix products, arithmetic and copies ran while one was open for 17% -> 0% of each run, Pallas kernels for 0% -> 0%
where the time goes in v2:
time: 43.8 us; the launch traced here: 43.5 us
  Pallas kernels  34.4 us (79%)
  local copies, waits for them, and re-layouts  8.39 us (19%)
  between operations  0.66 us (2%)
    pallas_call x1, Pallas kernels, per_device(): pl.pallas_call(functools.partial(kernel, dims, step), out_shape=[jax.Shap...  34.4 us
    unnamed x15, local copies, waits for them, and re-layouts  8.39 us

profile of v2, /device:TPU:0, one launch (start us, length us, event | category | flops | bytes accessed | tf_op | source)
XLA Modules:
  0.0 43.5 jit_solution(16069196658304479724)
XLA Ops:
  0.6 0.0 copy-start
  0.6 1.0 %copy-done = bf16[1,2,8,128,128]{4,3,2,1,0:T(8,128)(2,1)S(1)} copy-done((bf16[1,2,8,128,128]{4,3,2,1,0:T(8,128)(2,1)S(1)}, bf16[1,2,8,128,128]{4,3,2,1,0:T(8,128)(2,1)}, u32[]{:S(2)}) %copy-start) | copy-done | bytes 524312
  1.7 0.0 copy-start.1
  1.7 1.0 %copy-done.1 = bf16[3,3,128,128]{3,2,1,0:T(8,128)(2,1)S(1)} copy-done((bf16[3,3,128,128]{3,2,1,0:T(8,128)(2,1)S(1)}, bf16[3,3,128,128]{3,2,1,0:T(8,128)(2,1)}, u32[]{:S(2)}) %copy-start.1) | copy-done | bytes 294936
  2.6 0.0 copy-start.2
  2.6 0.9 %copy-done.2 = bf16[1,1,8,128,128]{4,3,2,1,0:T(8,128)(2,1)S(1)} copy-done((bf16[1,1,8,128,128]{4,3,2,1,0:T(8,128)(2,1)S(1)}, bf16[1,1,8,128,128]{4,3,2,1,0:T(8,128)(2,1)}, u32[]{:S(2)}) %copy-start.2) | copy-done | bytes 262168
  3.6 0.0 copy-start.3
  3.6 0.9 %copy-done.3 = bf16[3,128,128]{2,1,0:T(8,128)(2,1)S(1)} copy-done((bf16[3,128,128]{2,1,0:T(8,128)(2,1)S(1)}, bf16[3,128,128]{2,1,0:T(8,128)(2,1)}, u32[]{:S(2)}) %copy-start.3) | copy-done | bytes 98328
  4.5 0.0 copy-start.4
  4.5 0.9 %copy-done.4 = bf16[3,128,128]{2,1,0:T(8,128)(2,1)S(1)} copy-done((bf16[3,128,128]{2,1,0:T(8,128)(2,1)S(1)}, bf16[3,128,128]{2,1,0:T(8,128)(2,1)}, u32[]{:S(2)}) %copy-start.4) | copy-done | bytes 98328
  5.4 34.4 %shard_map.92 = (bf16[1,1,8,128,128]{4,3,2,1,0:T(8,128)(2,1)S(1)}, bf16[1,2,8,128,128]{4,3,2,1,0:T(8,128)(2,1)S(1)}, f32[3,3,128,128]{3,2,1,0:T(8,128)S(1)}, f32...) custom-call(bf16[1,2,8,128,128]{4,3,2,1,0:T(8,128)(2,1)S(1)} %copy-done, bf16[3,3,128,128]{3,2,1,0:T(8,128)(2,1)S(1)} %copy-done.1, ...), custom_call_target="tpu_custom_call" | custom-call | tf_op jit(solution)/shard_map/pallas_call | solution.py:370
  39.8 0.7 %copy.15 = bf16[1,1,8,128,128]{4,3,2,1,0:T(8,128)(2,1)} copy(bf16[1,1,8,128,128]{4,3,2,1,0:T(8,128)(2,1)S(1)} %get-tuple-element.10) | data formatting | bytes 524288
  40.5 0.8 %copy.16 = bf16[1,2,8,128,128]{4,3,2,1,0:T(8,128)(2,1)} copy(bf16[1,2,8,128,128]{4,3,2,1,0:T(8,128)(2,1)S(1)} %get-tuple-element.11) | data formatting | bytes 1048576
  41.3 0.8 %copy.17 = f32[3,3,128,128]{3,2,1,0:T(8,128)} copy(f32[3,3,128,128]{3,2,1,0:T(8,128)S(1)} %get-tuple-element.12) | data formatting | bytes 1179648
  42.1 0.7 %copy.18 = f32[3,128,128]{2,1,0:T(8,128)} copy(f32[3,128,128]{2,1,0:T(8,128)S(1)} %get-tuple-element.13) | data formatting | bytes 393216
  42.8 0.7 %copy.19 = f32[3,128,128]{2,1,0:T(8,128)} copy(f32[3,128,128]{2,1,0:T(8,128)S(1)} %get-tuple-element.14) | data formatting | bytes 393216
Async XLA Ops:
  0.6 1.0 %copy-start = (bf16[1,2,8,128,128]{4,3,2,1,0:T(8,128)(2,1)S(1)}, bf16[1,2,8,128,128]{4,3,2,1,0:T(8,128)(2,1)}, u32[]{:S(2)}) copy-start(bf16[1,2,8,128,128]{4,3,2,1,0:T(8,128)(2,1)} %x_ref.1) | copy-start | bytes 1572868
  1.7 1.0 %copy-start.1 = (bf16[3,3,128,128]{3,2,1,0:T(8,128)(2,1)S(1)}, bf16[3,3,128,128]{3,2,1,0:T(8,128)(2,1)}, u32[]{:S(2)}) copy-start(bf16[3,3,128,128]{3,2,1,0:T(8,128)(2,1)} %ws_ref.1) | copy-start | bytes 884740
  2.6 0.9 %copy-start.2 = (bf16[1,1,8,128,128]{4,3,2,1,0:T(8,128)(2,1)S(1)}, bf16[1,1,8,128,128]{4,3,2,1,0:T(8,128)(2,1)}, u32[]{:S(2)}) copy-start(bf16[1,1,8,128,128]{4,3,2,1,0:T(8,128)(2,1)} %c_ref.1) | copy-start | bytes 786436
  3.6 0.9 %copy-start.3 = (bf16[3,128,128]{2,1,0:T(8,128)(2,1)S(1)}, bf16[3,128,128]{2,1,0:T(8,128)(2,1)}, u32[]{:S(2)}) copy-start(bf16[3,128,128]{2,1,0:T(8,128)(2,1)} %wt_ref.1) | copy-start | bytes 294916
  4.5 0.9 %copy-start.4 = (bf16[3,128,128]{2,1,0:T(8,128)(2,1)S(1)}, bf16[3,128,128]{2,1,0:T(8,128)(2,1)}, u32[]{:S(2)}) copy-start(bf16[3,128,128]{2,1,0:T(8,128)(2,1)} %wd_ref.1) | copy-start | bytes 294916

commit v3 on v2

--- a/solution.py
+++ b/solution.py
@@ -173,34 +173,59 @@
 
 
 def kernel(
-    dims, step, x_ref, ws_ref, wt_ref, wd_ref, c_ref,
+    dims, step, x_hbm, ws_hbm, wt_hbm, wd_hbm, c_hbm,
     down_ref, gx_ref, os_ref, ot_ref, od_ref,
     xp, xt, gp, gcat, act, slope, gres, gb, cm, cp, lcat, part, d_out, e_out, d_in, e_in,
-    wf, wb, tcat, tflip, dflip, dback, edge_sems, *sums,
+    ws_ref, wt_ref, wd_ref, c_ref, wf, wb, tcat, tflip, dflip, dback, load_sems, edge_sems, *sums,
 ):
-    _, rows, width, ch = x_ref.shape[1:]
+    _, rows, width, ch = x_hbm.shape[1:]
+    cuts = rows // step
     tokens = rows * width
     per = step * width
     half = len(sums) // 2
     big, small = Sum(dims, 9, sums[:half]), Sum(dims, 6, sums[half:])
     edges = [
-        Edge(x_ref.at[0, :, rows - 1], xp.at[:, 0], edge_sems.at[0], "height", 1),
-        Edge(x_ref.at[0, :, 0], xp.at[:, rows + 1], edge_sems.at[1], "height", -1),
-        Edge(c_ref.at[0, 0], cm, edge_sems.at[2], "tm", 1),
-        Edge(c_ref.at[0, 0], cp, edge_sems.at[3], "tm", -1),
-        Edge(gp.at[:, rows], gp.at[:, 0], edge_sems.at[4], "height", 1),
-        Edge(gp.at[:, 1], gp.at[:, rows + 1], edge_sems.at[5], "height", -1),
-        Edge(d_out, d_in, edge_sems.at[6], "tm", 1),
-        Edge(e_out, e_in, edge_sems.at[7], "tm", -1),
+        Edge(x_hbm.at[0, :, rows - 1], xp.at[:, 0], edge_sems.at[0], "height", 1),
+        Edge(x_hbm.at[0, :, 0], xp.at[:, rows + 1], edge_sems.at[1], "height", -1),
+        Edge(gp.at[:, rows], gp.at[:, 0], edge_sems.at[2], "height", 1),
+        Edge(gp.at[:, 1], gp.at[:, rows + 1], edge_sems.at[3], "height", -1),
+        Edge(d_out, d_in, edge_sems.at[4], "tm", 1),
+        Edge(e_out, e_in, edge_sems.at[5], "tm", -1),
+    ]
+    near = []
+    for i in range(cuts):
+        at = pl.ds(i * step, step)
+        near.append(
+            (
+                Edge(c_hbm.at[0, 0, at], cm.at[at], edge_sems.at[6 + 2 * i], "tm", 1),
+                Edge(c_hbm.at[0, 0, at], cp.at[at], edge_sems.at[7 + 2 * i], "tm", -1),
+            )
+        )
+    loads = [
+        pltpu.make_async_copy(src, dst, load_sems.at[i])
+        for i, (src, dst) in enumerate(
+            (
+                (ws_hbm, ws_ref),
+                (x_hbm.at[0], xp.at[:, pl.ds(1, rows)]),
+                (wt_hbm, wt_ref),
+                (wd_hbm, wd_ref),
+                (c_hbm, c_ref),
+            )
+        )
     ]
     inner = (lax.axis_index("tm") > 0).astype(jnp.float32)
     col = lax.broadcasted_iota(jnp.int32, (step, width, ch), 1).reshape(per, ch)
 
+    for copy in loads:
+        copy.start()
     greet(dims)
-    for e in edges[:4]:
+    for e in edges[:2]:
         e.start()
-    for f in range(2):
-        xp[f, pl.ds(1, rows)] = x_ref[0, f]
+    for pair in near:
+        for e in pair:
+            e.start()
+    for copy in loads:
+        copy.wait()
     for k in range(3):
         tcat[:, (2 - k) * ch : (3 - k) * ch] = wt_ref[k]
         tflip[k * ch : (k + 1) * ch, :] = wt_ref[k].T
@@ -227,9 +252,10 @@
             + from_right(out[:, 2 * ch :], col, width)
         )
 
+    for f in range(2):
+        xt[f, :, width : (rows + 1) * width] = xp[f, pl.ds(1, rows)].reshape(tokens, ch).T
     for e in edges[:2]:
         e.arrive()
-    cuts = rows // step
 
     def forward(i, carry):
         f, y = i // cuts, (i % cuts) * step
@@ -242,12 +268,33 @@
     lax.fori_loop(0, 2 * cuts, forward, 0)
 
     for f in range(2):
-        xt[f] = xp[f].reshape((rows + 2) * width, ch).T
-
-    for e in edges[2:4]:
-        e.arrive()
-
-    def backward(i, carry):
+        xt[f, :, :width] = xp[f, 0].T
+        xt[f, :, (rows + 1) * width :] = xp[f, rows + 1].T
+
+    def mixing(i, carry):
+        at = pl.ds(i * step, step)
+        y0 = dot(flat(act[0, at]), tcat[...])
+        y1 = dot(flat(act[1, at]), tcat[...])
+        x0 = flat(xp[0, pl.ds(i * step + 1, step)]).astype(jnp.float32)
+        x1 = flat(xp[1, pl.ds(i * step + 1, step)]).astype(jnp.float32)
+        l0 = (y0[:, :ch] * inner).astype(jnp.bfloat16)
+        l1 = (x0 + y0[:, ch : 2 * ch] + y1[:, :ch]).astype(jnp.bfloat16)
+        l2 = (x1 + y0[:, 2 * ch :] + y1[:, ch : 2 * ch]).astype(jnp.bfloat16)
+        u = y1[:, 2 * ch :].astype(jnp.bfloat16)
+        for n, v in enumerate((l0, l1, l2, u)):
+            lcat[n, at] = tall(v)
+        own = jnp.concatenate([l0, l1, l2], axis=1)
+        part[at] = tall(dot(own, wd_ref[...].reshape(3 * ch, ch)))
+        ahead = jnp.concatenate([l2, u], axis=1)
+        d_out[at] = tall(dot(ahead, wd_ref[0:2].reshape(2 * ch, ch)).astype(jnp.bfloat16))
+        e_out[at] = tall(dot(l0, wd_ref[2]).astype(jnp.bfloat16))
+        return carry
+
+    lax.fori_loop(0, cuts, mixing, 0)
+    for e in edges[4:]:
+        e.start()
+
+    def backward(i):
         at = pl.ds(i * step, step)
         c0, before, after = flat(c_ref[0, 0, at]), flat(cm[at]), flat(cp[at])
         g0 = dot(jnp.concatenate([before, c0], axis=1), dback[...]) * inner
@@ -267,10 +314,12 @@
             gcat[a, at, :, :ch] = tall(from_right(gpre, col, width).astype(jnp.bfloat16))
             gcat[a, at, :, ch : 2 * ch] = tall(low)
             gcat[a, at, :, 2 * ch :] = tall(from_left(gpre, col).astype(jnp.bfloat16))
-        return carry
-
-    lax.fori_loop(0, cuts, backward, 0)
-    for e in edges[4:6]:
+
+    for i in range(cuts):
+        for e in near[i]:
+            e.arrive()
+        backward(i)
+    for e in edges[2:4]:
         e.start()
 
     total = jnp.zeros((3 * ch, 3 * ch), jnp.float32)
@@ -286,29 +335,6 @@
             ].astype(jnp.bfloat16)
     big.start()
 
-    def mixing(i, carry):
-        at = pl.ds(i * step, step)
-        y0 = dot(flat(act[0, at]), tcat[...])
-        y1 = dot(flat(act[1, at]), tcat[...])
-        x0 = flat(x_ref[0, 0, at]).astype(jnp.float32)
-        x1 = flat(x_ref[0, 1, at]).astype(jnp.float32)
-        l0 = (y0[:, :ch] * inner).astype(jnp.bfloat16)
-        l1 = (x0 + y0[:, ch : 2 * ch] + y1[:, :ch]).astype(jnp.bfloat16)
-        l2 = (x1 + y0[:, 2 * ch :] + y1[:, ch : 2 * ch]).astype(jnp.bfloat16)
-        u = y1[:, 2 * ch :].astype(jnp.bfloat16)
-        for n, v in enumerate((l0, l1, l2, u)):
-            lcat[n, at] = tall(v)
-        own = jnp.concatenate([l0, l1, l2], axis=1)
-        part[at] = tall(dot(own, wd_ref[...].reshape(3 * ch, ch)))
-        ahead = jnp.concatenate([l2, u], axis=1)
-        d_out[at] = tall(dot(ahead, wd_ref[0:2].reshape(2 * ch, ch)).astype(jnp.bfloat16))
-        e_out[at] = tall(dot(l0, wd_ref[2]).astype(jnp.bfloat16))
-        return carry
-
-    lax.fori_loop(0, cuts, mixing, 0)
-    for e in edges[6:]:
-        e.start()
-
     times = jnp.zeros((ch, 3 * ch), jnp.float32)
     for a in range(2):
         wide = jnp.concatenate([gb[n].reshape(tokens, ch) for n in (a + 2, a + 1, a)], axis=1)
@@ -327,7 +353,7 @@
     small.start()
 
     big.middle()
-    for e in edges[4:6]:
+    for e in edges[2:4]:
         e.arrive()
 
     def features(f):
@@ -344,7 +370,7 @@
     big.last()
     features(1)
     small.last()
-    for e in edges[6:]:
+    for e in edges[4:]:
         e.arrive()
     down_ref[0, 0] = (
         part[...] + d_in[...].astype(jnp.float32) + e_in[...].astype(jnp.float32)
@@ -358,25 +384,39 @@
         od_ref[i] = small.full[pl.ds((3 + i) * ch, ch)].astype(jnp.float32)
     for e in edges:
         e.leave()
+    for pair in near:
+        for e in pair:
+            e.leave()
+
+
+def store(*refs):
+    sems = refs[-1]
+    copies = [pltpu.make_async_copy(refs[i], refs[5 + i], sems.at[i]) for i in range(5)]
+    for copy in copies:
+        copy.start()
+    for copy in copies:
+        copy.wait()
 
 
 def per_device(features, w_spatial, w_temporal, w_down, cotangent):
+    args = (features, w_spatial, w_temporal, w_down, cotangent)
     dims = tuple(lax.axis_size(a) for a in AXES)
     _, frames, rows, width, ch = features.shape
     peers = dims[0] * dims[2]
     step = 4
     bf, f32 = jnp.bfloat16, jnp.float32
     frame = (rows, width, ch)
-    return pl.pallas_call(
+    shapes = [
+        jax.ShapeDtypeStruct(cotangent.shape, bf),
+        jax.ShapeDtypeStruct(features.shape, bf),
+        jax.ShapeDtypeStruct(w_spatial.shape, f32),
+        jax.ShapeDtypeStruct(w_temporal.shape, f32),
+        jax.ShapeDtypeStruct(w_down.shape, f32),
+    ]
+    outs = pl.pallas_call(
         functools.partial(kernel, dims, step),
-        out_shape=[
-            jax.ShapeDtypeStruct(cotangent.shape, bf),
-            jax.ShapeDtypeStruct(features.shape, bf),
-            jax.ShapeDtypeStruct(w_spatial.shape, f32),
-            jax.ShapeDtypeStruct(w_temporal.shape, f32),
-            jax.ShapeDtypeStruct(w_down.shape, f32),
-        ],
-        in_specs=[pl.BlockSpec(memory_space=pltpu.VMEM)] * 5,
+        out_shape=shapes,
+        in_specs=[pl.BlockSpec(memory_space=pltpu.HBM)] * 5,
         out_specs=[pl.BlockSpec(memory_space=pltpu.VMEM)] * 5,
         scratch_shapes=[
             pltpu.VMEM((2, rows + 2, width, ch), bf),
@@ -395,20 +435,32 @@
             pltpu.VMEM(frame, bf),
             pltpu.VMEM(frame, bf),
             pltpu.VMEM(frame, bf),
+            pltpu.VMEM(w_spatial.shape, bf),
+            pltpu.VMEM(w_temporal.shape, bf),
+            pltpu.VMEM(w_down.shape, bf),
+            pltpu.VMEM(cotangent.shape, bf),
             pltpu.VMEM((3 * ch, 3 * ch), bf),
             pltpu.VMEM((3 * ch, 3 * ch), bf),
             pltpu.VMEM((ch, 3 * ch), bf),
             pltpu.VMEM((3 * ch, ch), bf),
             pltpu.VMEM((ch, 3 * ch), bf),
             pltpu.VMEM((2 * ch, ch), bf),
-            pltpu.SemaphoreType.DMA((8, 2)),
+            pltpu.SemaphoreType.DMA((5,)),
+            pltpu.SemaphoreType.DMA((6 + 2 * rows // step, 2)),
         ]
         + sum_scratch(9, peers, dims[1])
         + sum_scratch(6, peers, dims[1]),
         compiler_params=pltpu.CompilerParams(
             collective_id=0, has_side_effects=True, vmem_limit_bytes=40 * 1024 * 1024
         ),
-    )(features, w_spatial, w_temporal, w_down, cotangent)
+    )(*(pltpu.with_memory_space_constraint(v, pltpu.HBM) for v in args))
+    return pl.pallas_call(
+        store,
+        out_shape=shapes,
+        in_specs=[pl.BlockSpec(memory_space=pltpu.VMEM)] * 5,
+        out_specs=[pl.BlockSpec(memory_space=pltpu.HBM)] * 5,
+        scratch_shapes=[pltpu.SemaphoreType.DMA((5,))],
+    )(*outs)
 
 
 def solution(mesh):

time: 43.8 us -> 40.8 us (0.932)
  local copies, waits for them, and re-layouts: 8.39 us -> 3.65 us
  Pallas kernels: 34.4 us -> 36.3 us
    unnamed x15 -> x10, local copies, waits for them, and re-layouts: 8.39 us -> 3.65 us
    pallas_call x1 -> x2, Pallas kernels: 34.4 us -> 36.3 us  [the longest x1 33.7 us: per_device(): pl.pallas_call(functools.partial(kernel, dims, step), out_shape=shapes, i...]
where the time goes in v3:
time: 40.8 us; the launch traced here: 40.6 us
  Pallas kernels  36.3 us (89%)
  local copies, waits for them, and re-layouts  3.65 us (9%)
  between operations  0.65 us (2%)
    pallas_call x1, Pallas kernels, per_device(): pl.pallas_call(functools.partial(kernel, dims, step), out_shape=shapes, i...  33.7 us
    unnamed x10, local copies, waits for them, and re-layouts  3.65 us
    pallas_call x1, Pallas kernels, per_device(): pl.pallas_call(store, out_shape=shapes, in_specs=[pl.BlockSpec(memory_spa...  2.64 us

profile of v3, /device:TPU:0, one launch (start us, length us, event | category | flops | bytes accessed | tf_op | source)
XLA Modules:
  0.0 40.6 jit_solution(1783419188506801164)
XLA Ops:
  0.6 33.7 %shard_map.92 = (bf16[1,1,8,128,128]{4,3,2,1,0:T(8,128)(2,1)S(1)}, bf16[1,2,8,128,128]{4,3,2,1,0:T(8,128)(2,1)S(1)}, f32[3,3,128,128]{3,2,1,0:T(8,128)S(1)}, f32...) custom-call(bf16[1,2,8,128,128]{4,3,2,1,0:T(8,128)(2,1)} %x_hbm.1, bf16[3,3,128,128]{3,2,1,0:T(8,128)(2,1)} %ws_hbm.1, ...), custom_call_target="tpu_custom_call" | custom-call | tf_op jit(solution)/shard_map/pallas_call | solution.py:416
  34.3 0.0 copy-start
  34.3 0.8 %copy-done = f32[3,3,128,128]{3,2,1,0:T(8,128)} copy-done((f32[3,3,128,128]{3,2,1,0:T(8,128)}, f32[3,3,128,128]{3,2,1,0:T(8,128)S(1)}, u32[]{:S(2)}) %copy-start) | copy-done | bytes 589848
  35.1 0.0 copy-start.1
  35.1 0.8 %copy-done.1 = bf16[1,2,8,128,128]{4,3,2,1,0:T(8,128)(2,1)} copy-done((bf16[1,2,8,128,128]{4,3,2,1,0:T(8,128)(2,1)}, bf16[1,2,8,128,128]{4,3,2,1,0:T(8,128)(2,1)S(1)}, u32[]{:S(2)}) %copy-start.1) | copy-done | bytes 524312
  35.9 0.0 copy-start.2
  35.9 0.7 %copy-done.2 = bf16[1,1,8,128,128]{4,3,2,1,0:T(8,128)(2,1)} copy-done((bf16[1,1,8,128,128]{4,3,2,1,0:T(8,128)(2,1)}, bf16[1,1,8,128,128]{4,3,2,1,0:T(8,128)(2,1)S(1)}, u32[]{:S(2)}) %copy-start.2) | copy-done | bytes 262168
  36.6 0.0 copy-start.3
  36.6 0.7 %copy-done.3 = f32[3,128,128]{2,1,0:T(8,128)} copy-done((f32[3,128,128]{2,1,0:T(8,128)}, f32[3,128,128]{2,1,0:T(8,128)S(1)}, u32[]{:S(2)}) %copy-start.3) | copy-done | bytes 196632
  37.3 0.0 copy-start.4
  37.3 0.7 %copy-done.4 = f32[3,128,128]{2,1,0:T(8,128)} copy-done((f32[3,128,128]{2,1,0:T(8,128)}, f32[3,128,128]{2,1,0:T(8,128)S(1)}, u32[]{:S(2)}) %copy-start.4) | copy-done | bytes 196632
  38.0 2.6 %shard_map.93 = (bf16[1,1,8,128,128]{4,3,2,1,0:T(8,128)(2,1)}, bf16[1,2,8,128,128]{4,3,2,1,0:T(8,128)(2,1)}, f32[3,3,128,128]{3,2,1,0:T(8,128)}, f32[3,128,128]{2,1,0:T(8,128)}, f32[3,128,128]{2,1,0:T(8,128)}) custom-call(bf16[1,1,8,128,128]{4,3,2,1,0:T(8,128)(2,1)} %copy-done.2, bf16[1,2,8,128,128]{4,3,2,1,0:T(8,128)(2,1)} %copy-done.1, ...), custom_call_target="tpu_custom_call" | custom-call | tf_op jit(solution)/shard_map/pallas_call | solution.py:457
Async XLA Ops:
  34.3 0.8 %copy-start = (f32[3,3,128,128]{3,2,1,0:T(8,128)}, f32[3,3,128,128]{3,2,1,0:T(8,128)S(1)}, u32[]{:S(2)}) copy-start(f32[3,3,128,128]{3,2,1,0:T(8,128)S(1)} %get-tuple-element.12.refs_2_) | copy-start | bytes 1769476
  35.1 0.8 %copy-start.1 = (bf16[1,2,8,128,128]{4,3,2,1,0:T(8,128)(2,1)}, bf16[1,2,8,128,128]{4,3,2,1,0:T(8,128)(2,1)S(1)}, u32[]{:S(2)}) copy-start(bf16[1,2,8,128,128]{4,3,2,1,0:T(8,128)(2,1)S(1)} %get-tuple-element.11.refs_1_) | copy-start | bytes 1572868
  35.9 0.7 %copy-start.2 = (bf16[1,1,8,128,128]{4,3,2,1,0:T(8,128)(2,1)}, bf16[1,1,8,128,128]{4,3,2,1,0:T(8,128)(2,1)S(1)}, u32[]{:S(2)}) copy-start(bf16[1,1,8,128,128]{4,3,2,1,0:T(8,128)(2,1)S(1)} %get-tuple-element.10.refs_0_) | copy-start | bytes 786436
  36.6 0.7 %copy-start.3 = (f32[3,128,128]{2,1,0:T(8,128)}, f32[3,128,128]{2,1,0:T(8,128)S(1)}, u32[]{:S(2)}) copy-start(f32[3,128,128]{2,1,0:T(8,128)S(1)} %get-tuple-element.13.refs_3_) | copy-start | bytes 589828
  37.3 0.7 %copy-start.4 = (f32[3,128,128]{2,1,0:T(8,128)}, f32[3,128,128]{2,1,0:T(8,128)S(1)}, u32[]{:S(2)}) copy-start(f32[3,128,128]{2,1,0:T(8,128)S(1)} %get-tuple-element.14.refs_4_) | copy-start | bytes 589828

commit v4 on v3

--- a/solution.py
+++ b/solution.py
@@ -17,12 +17,16 @@
 
 def sum_scratch(mats, peers, depth):
     rows = rows_each(mats, peers)
+    half = peers // 2 * rows
     return [
-        pltpu.VMEM((peers * rows, 128), jnp.bfloat16),
-        pltpu.VMEM((peers * rows, 128), jnp.bfloat16),
+        pltpu.VMEM((2 * half, 128), jnp.float32),
+        pltpu.VMEM((half, 128), jnp.bfloat16),
+        pltpu.VMEM((half, 128), jnp.bfloat16),
+        pltpu.VMEM((half, 128), jnp.bfloat16),
+        pltpu.VMEM((half, 128), jnp.bfloat16),
         pltpu.VMEM((depth * rows, 128), jnp.bfloat16),
-        pltpu.VMEM((peers * rows, 128), jnp.bfloat16),
-        pltpu.SemaphoreType.DMA((3, 2, max(peers, depth))),
+        pltpu.VMEM((2 * half, 128), jnp.bfloat16),
+        pltpu.SemaphoreType.DMA((5, 2, max(peers // 2, depth))),
     ]
 
 
@@ -30,65 +34,81 @@
     def __init__(self, dims, mats, refs):
         self.nb, self.nz, self.nh = dims
         self.mats = mats
-        self.peers = self.nb * self.nh
-        self.rows = rows_each(mats, self.peers)
-        self.out, self.got, self.deep, self.full, self.sems = refs
+        self.rows = rows_each(mats, self.nb * self.nh)
+        self.out, self.give, self.take, self.send, self.got, self.deep, self.full, self.sems = refs
         self.b, self.z, self.h = (lax.axis_index(a) for a in AXES)
-        self.me = self.b * self.nh + self.h
+        self.wide = self.nh // 2
+        self.chips = self.nb * self.wide
+        self.core = lax.rem(self.h, 2)
+        self.me = self.b * self.wide + self.h // 2
 
     def slot(self, i):
         return pl.ds(pl.multiple_of(i * self.rows, 16), self.rows)
 
-    def plane(self, o):
-        p = lax.rem(self.me + o, self.peers)
-        return p, (p // self.nh, self.z, lax.rem(p, self.nh))
-
-    def scatter(self, o):
-        p, dev = self.plane(o)
+    def half(self, core):
+        size = self.chips * self.rows
+        return pl.ds(pl.multiple_of(core * size, 16), size)
+
+    def copy(self, src, dst, stage, n, dev):
         return pltpu.make_async_remote_copy(
-            src_ref=self.out.at[self.slot(p)],
-            dst_ref=self.got.at[self.slot(self.me)],
-            send_sem=self.sems.at[0, 0, o],
-            recv_sem=self.sems.at[0, 1, o],
+            src_ref=src,
+            dst_ref=dst,
+            send_sem=self.sems.at[stage, 0, n],
+            recv_sem=self.sems.at[stage, 1, n],
             device_id=dev,
             device_id_type=MESH,
         )
 
+    def partner(self):
+        return (self.b, self.z, self.h + 1 - 2 * self.core)
+
+    def chip(self, o):
+        p = lax.rem(self.me + o, self.chips)
+        return p, (p // self.wide, self.z, lax.rem(p, self.wide) * 2 + self.core)
+
+    def behind(self, o):
+        return lax.rem(self.me - o + self.chips, self.chips)
+
+    def swap(self):
+        return self.copy(self.give, self.take, 0, 0, self.partner())
+
+    def scatter(self, o):
+        p, dev = self.chip(o)
+        return self.copy(self.send.at[self.slot(p)], self.got.at[self.slot(self.me)], 1, o, dev)
+
     def along(self, o):
         q = lax.rem(self.z + o, self.nz)
-        return pltpu.make_async_remote_copy(
-            src_ref=self.deep.at[self.slot(self.z)],
-            dst_ref=self.deep.at[self.slot(self.z)],
-            send_sem=self.sems.at[1, 0, o],
-            recv_sem=self.sems.at[1, 1, o],
-            device_id=(self.b, q, self.h),
-            device_id_type=MESH,
-        )
+        mine = self.deep.at[self.slot(self.z)]
+        return self.copy(mine, mine, 2, o, (self.b, q, self.h))
 
     def gather(self, o):
-        _, dev = self.plane(o)
-        return pltpu.make_async_remote_copy(
-            src_ref=self.full.at[self.slot(self.me)],
-            dst_ref=self.full.at[self.slot(self.me)],
-            send_sem=self.sems.at[2, 0, o],
-            recv_sem=self.sems.at[2, 1, o],
-            device_id=dev,
-            device_id_type=MESH,
-        )
+        _, dev = self.chip(o)
+        mine = self.full.at[self.slot(self.core * self.chips + self.me)]
+        return self.copy(mine, mine, 3, o, dev)
+
+    def forward(self, o):
+        piece = self.full.at[self.slot(self.core * self.chips + self.behind(o))]
+        return self.copy(piece, piece, 4, o, self.partner())
+
+    def pair(self):
+        pad = 2 * self.chips * self.rows - self.mats * 128
+        if pad:
+            self.out[pl.ds(self.mats * 128, pad)] = jnp.zeros((pad, 128), jnp.float32)
+        self.give[...] = self.out[self.half(1 - self.core)].astype(jnp.bfloat16)
+        self.swap().start()
 
     def start(self):
-        pad = self.peers * self.rows - self.mats * 128
-        if pad:
-            self.out[pl.ds(self.mats * 128, pad)] = jnp.zeros((pad, 128), jnp.bfloat16)
-        for o in range(1, self.peers):
+        self.swap().wait()
+        total = self.out[self.half(self.core)] + self.take[...].astype(jnp.float32)
+        self.send[...] = total.astype(jnp.bfloat16)
+        for o in range(1, self.chips):
             self.scatter(o).start()
 
     def middle(self):
-        total = self.out[self.slot(self.me)].astype(jnp.float32)
-        for o in range(1, self.peers):
+        total = self.send[self.slot(self.me)].astype(jnp.float32)
+        for o in range(1, self.chips):
             self.scatter(o).wait()
-            src = lax.rem(self.me - o + self.peers, self.peers)
-            total = total + self.got[self.slot(src)].astype(jnp.float32)
+            total = total + self.got[self.slot(self.behind(o))].astype(jnp.float32)
         self.deep[self.slot(self.z)] = total.astype(jnp.bfloat16)
         for o in range(1, self.nz):
             self.along(o).start()
@@ -99,13 +119,18 @@
         total = self.deep[pl.ds(0, self.rows)].astype(jnp.float32)
         for q in range(1, self.nz):
             total = total + self.deep[pl.ds(q * self.rows, self.rows)].astype(jnp.float32)
-        self.full[self.slot(self.me)] = total.astype(jnp.bfloat16)
-        for o in range(1, self.peers):
+        mine = self.slot(self.core * self.chips + self.me)
+        self.full[mine] = total.astype(jnp.bfloat16)
+        for o in range(1, self.chips):
             self.gather(o).start()
+        self.forward(0).start()
 
     def finish(self):
-        for o in range(1, self.peers):
+        for o in range(1, self.chips):
             self.gather(o).wait()
+            self.forward(o).start()
+        for o in range(self.chips):
+            self.forward(o).wait()
 
 
 def greet(dims):
@@ -332,13 +357,14 @@
         for dx in range(3):
             big.out[pl.ds((dy * 3 + dx) * ch, ch)] = total[
                 dy * ch : (dy + 1) * ch, dx * ch : (dx + 1) * ch
-            ].astype(jnp.bfloat16)
-    big.start()
+            ]
+    big.pair()
 
     times = jnp.zeros((ch, 3 * ch), jnp.float32)
     for a in range(2):
         wide = jnp.concatenate([gb[n].reshape(tokens, ch) for n in (a + 2, a + 1, a)], axis=1)
         times = times + dot(act[a].reshape(tokens, ch).T, wide)
+    big.start()
     left = jnp.concatenate([lcat[n].reshape(tokens, ch).T for n in range(4)], axis=0)
     wide = jnp.concatenate([v.reshape(tokens, ch) for v in (cp[...], c_ref[0, 0], cm[...])], axis=1)
     outer = dot(left, wide)
@@ -348,11 +374,9 @@
 
     downs = (block(2, 0) + block(0, 1), block(1, 1) + block(3, 0), block(2, 1) + block(0, 2))
     for k in range(3):
-        small.out[pl.ds(k * ch, ch)] = times[:, k * ch : (k + 1) * ch].astype(jnp.bfloat16)
-        small.out[pl.ds((3 + k) * ch, ch)] = downs[k].astype(jnp.bfloat16)
-    small.start()
-
-    big.middle()
+        small.out[pl.ds(k * ch, ch)] = times[:, k * ch : (k + 1) * ch]
+        small.out[pl.ds((3 + k) * ch, ch)] = downs[k]
+    small.pair()
     for e in edges[2:4]:
         e.arrive()
 
@@ -366,15 +390,17 @@
         lax.fori_loop(0, cuts, body, 0)
 
     features(0)
+    small.start()
+    big.middle()
+    features(1)
     small.middle()
     big.last()
-    features(1)
-    small.last()
     for e in edges[4:]:
         e.arrive()
     down_ref[0, 0] = (
         part[...] + d_in[...].astype(jnp.float32) + e_in[...].astype(jnp.float32)
     ).astype(jnp.bfloat16)
+    small.last()
     big.finish()
     for i in range(9):
         os_ref[i // 3, i % 3] = big.full[pl.ds(i * ch, ch)].astype(jnp.float32)
@@ -460,6 +486,7 @@
         in_specs=[pl.BlockSpec(memory_space=pltpu.VMEM)] * 5,
         out_specs=[pl.BlockSpec(memory_space=pltpu.HBM)] * 5,
         scratch_shapes=[pltpu.SemaphoreType.DMA((5,))],
+        compiler_params=pltpu.CompilerParams(vmem_limit_bytes=4 * 1024 * 1024),
     )(*outs)
 
 

time: 40.8 us -> 34.6 us (0.85)
  local copies, waits for them, and re-layouts: 3.65 us -> 0 us
  Pallas kernels: 36.3 us -> 33.9 us
    unnamed x10 -> x0, local copies, waits for them, and re-layouts: 3.65 us -> none
    pallas_call x1, Pallas kernels: 2.64 us -> 1.24 us  [per_device(): pl.pallas_call(store, out_shape=shapes, in_specs=[pl.BlockSpec(memory_spa...]
    pallas_call x1, Pallas kernels: 33.7 us -> 32.6 us  [per_device(): pl.pallas_call(functools.partial(kernel, dims, step), out_shape=shapes, i...]
where the time goes in v4:
time: 34.6 us; the launch traced here: 34.5 us
  Pallas kernels  33.9 us (98%)
  between operations  0.64 us (2%)
    pallas_call x1, Pallas kernels, per_device(): pl.pallas_call(functools.partial(kernel, dims, step), out_shape=shapes, i...  32.6 us
    pallas_call x1, Pallas kernels, per_device(): pl.pallas_call(store, out_shape=shapes, in_specs=[pl.BlockSpec(memory_spa...  1.24 us

profile of v4, /device:TPU:0, one launch (start us, length us, event | category | flops | bytes accessed | tf_op | source)
XLA Modules:
  0.0 34.5 jit_solution(13730292415971617326)
XLA Ops:
  0.6 32.6 %shard_map.92 = (bf16[1,1,8,128,128]{4,3,2,1,0:T(8,128)(2,1)S(1)}, bf16[1,2,8,128,128]{4,3,2,1,0:T(8,128)(2,1)S(1)}, f32[3,3,128,128]{3,2,1,0:T(8,128)S(1)}, f32...) custom-call(bf16[1,2,8,128,128]{4,3,2,1,0:T(8,128)(2,1)} %x_hbm.1, bf16[3,3,128,128]{3,2,1,0:T(8,128)(2,1)} %ws_hbm.1, ...), custom_call_target="tpu_custom_call" | custom-call | tf_op jit(solution)/shard_map/pallas_call | solution.py:442
  33.3 1.2 %shard_map.93 = (bf16[1,1,8,128,128]{4,3,2,1,0:T(8,128)(2,1)}, bf16[1,2,8,128,128]{4,3,2,1,0:T(8,128)(2,1)}, f32[3,3,128,128]{3,2,1,0:T(8,128)}, f32[3,128,128]{2,1,0:T(8,128)}, f32[3,128,128]{2,1,0:T(8,128)}) custom-call(bf16[1,1,8,128,128]{4,3,2,1,0:T(8,128)(2,1)S(1)} %get-tuple-element.10.refs_0_, ...), custom_call_target="tpu_custom_call" | custom-call | tf_op jit(solution)/shard_map/pallas_call | solution.py:483

commit v5 on v4

--- a/solution.py
+++ b/solution.py
@@ -200,7 +200,7 @@
 def kernel(
     dims, step, x_hbm, ws_hbm, wt_hbm, wd_hbm, c_hbm,
     down_ref, gx_ref, os_ref, ot_ref, od_ref,
-    xp, xt, gp, gcat, act, slope, gres, gb, cm, cp, lcat, part, d_out, e_out, d_in, e_in,
+    xp, xt, gp, gcat, act, slope, gres, gb, cm, cp, lcat, ct, part, d_out, e_out, d_in, e_in,
     ws_ref, wt_ref, wd_ref, c_ref, wf, wb, tcat, tflip, dflip, dback, load_sems, edge_sems, *sums,
 ):
     _, rows, width, ch = x_hbm.shape[1:]
@@ -251,47 +251,58 @@
             e.start()
     for copy in loads:
         copy.wait()
+    for dy in range(3):
+        for dx in range(3):
+            wf[dy * ch : (dy + 1) * ch, dx * ch : (dx + 1) * ch] = ws_ref[dy, dx]
+
+    def flat(v):
+        return v.reshape(per, ch)
+
+    def tall(v):
+        return v.reshape(step, width, ch)
+
+    def conv(ref, f, starts, count, weights):
+        def tap(dy):
+            pieces = [ref[f, pl.ds(y + dy, count)].reshape(count * width, ch) for y in starts]
+            return jnp.concatenate(pieces, axis=0)
+
+        out = dot(jnp.concatenate([tap(dy) for dy in range(3)], axis=1), weights[...])
+        return (
+            out[:, ch : 2 * ch]
+            + from_left(out[:, :ch], col)
+            + from_right(out[:, 2 * ch :], col, width)
+        )
+
+    def spread(ref, f, starts, count, v):
+        for n, y in enumerate(starts):
+            piece = v[n * count * width : (n + 1) * count * width]
+            ref[f, pl.ds(y, count)] = piece.reshape(count, width, ch)
+
+    inside = [((y,), step) for y in range(2, rows - 2, step)]
+    border = ((0, rows - 2), 2)
+
+    def forward(f, starts, count):
+        pre = conv(xp, f, starts, count, wf)
+        sig = jax.nn.sigmoid(pre)
+        spread(act, f, starts, count, (pre * sig).astype(jnp.bfloat16))
+        spread(slope, f, starts, count, sig * (1.0 + pre * (1.0 - sig)))
+
+    for f in range(2):
+        for cut in inside:
+            forward(f, *cut)
+    for f in range(2):
+        xt[f, :, width : (rows + 1) * width] = xp[f, pl.ds(1, rows)].reshape(tokens, ch).T
     for k in range(3):
         tcat[:, (2 - k) * ch : (3 - k) * ch] = wt_ref[k]
         tflip[k * ch : (k + 1) * ch, :] = wt_ref[k].T
         dflip[:, k * ch : (k + 1) * ch] = wd_ref[k].T
-        for dx in range(3):
-            w = ws_ref[k, dx]
-            wf[k * ch : (k + 1) * ch, dx * ch : (dx + 1) * ch] = w
-            wb[(2 - k) * ch : (3 - k) * ch, (2 - dx) * ch : (3 - dx) * ch] = w.T
     dback[0:ch, :] = dflip[:, 2 * ch : 3 * ch]
     dback[ch : 2 * ch, :] = dflip[:, 0:ch]
 
-    def flat(v):
-        return v.reshape(per, ch)
-
-    def tall(v):
-        return v.reshape(step, width, ch)
-
-    def conv(ref, f, y, weights):
-        wide = jnp.concatenate([flat(ref[f, pl.ds(y + dy, step)]) for dy in range(3)], axis=1)
-        out = dot(wide, weights[...])
-        return (
-            out[:, ch : 2 * ch]
-            + from_left(out[:, :ch], col)
-            + from_right(out[:, 2 * ch :], col, width)
-        )
-
-    for f in range(2):
-        xt[f, :, width : (rows + 1) * width] = xp[f, pl.ds(1, rows)].reshape(tokens, ch).T
     for e in edges[:2]:
         e.arrive()
-
-    def forward(i, carry):
-        f, y = i // cuts, (i % cuts) * step
-        pre = conv(xp, f, y, wf)
-        sig = jax.nn.sigmoid(pre)
-        act[f, pl.ds(y, step)] = tall((pre * sig).astype(jnp.bfloat16))
-        slope[f, pl.ds(y, step)] = tall(sig * (1.0 + pre * (1.0 - sig)))
-        return carry
-
-    lax.fori_loop(0, 2 * cuts, forward, 0)
-
+    for f in range(2):
+        forward(f, *border)
     for f in range(2):
         xt[f, :, :width] = xp[f, 0].T
         xt[f, :, (rows + 1) * width :] = xp[f, rows + 1].T
@@ -318,6 +329,8 @@
     lax.fori_loop(0, cuts, mixing, 0)
     for e in edges[4:]:
         e.start()
+
+    ct[ch : 2 * ch, :] = c_ref[0, 0].reshape(tokens, ch).T
 
     def backward(i):
         at = pl.ds(i * step, step)
@@ -365,29 +378,31 @@
         wide = jnp.concatenate([gb[n].reshape(tokens, ch) for n in (a + 2, a + 1, a)], axis=1)
         times = times + dot(act[a].reshape(tokens, ch).T, wide)
     big.start()
-    left = jnp.concatenate([lcat[n].reshape(tokens, ch).T for n in range(4)], axis=0)
-    wide = jnp.concatenate([v.reshape(tokens, ch) for v in (cp[...], c_ref[0, 0], cm[...])], axis=1)
-    outer = dot(left, wide)
+    ct[0:ch, :] = cp[...].reshape(tokens, ch).T
+    ct[2 * ch :, :] = cm[...].reshape(tokens, ch).T
+    wide = jnp.concatenate([lcat[n].reshape(tokens, ch) for n in range(4)], axis=1)
+    outer = dot(ct[...], wide)
 
     def block(n, m):
-        return outer[n * ch : (n + 1) * ch, m * ch : (m + 1) * ch]
+        return outer[m * ch : (m + 1) * ch, n * ch : (n + 1) * ch]
 
     downs = (block(2, 0) + block(0, 1), block(1, 1) + block(3, 0), block(2, 1) + block(0, 2))
     for k in range(3):
         small.out[pl.ds(k * ch, ch)] = times[:, k * ch : (k + 1) * ch]
-        small.out[pl.ds((3 + k) * ch, ch)] = downs[k]
+        small.out[pl.ds((3 + k) * ch, ch)] = downs[k].T
     small.pair()
+    for dy in range(3):
+        for dx in range(3):
+            at = slice((2 - dy) * ch, (3 - dy) * ch), slice((2 - dx) * ch, (3 - dx) * ch)
+            wb[at] = ws_ref[dy, dx].T
     for e in edges[2:4]:
         e.arrive()
 
     def features(f):
-        def body(i, carry):
-            at = pl.ds(i * step, step)
-            out = conv(gp, f, i * step, wb) + flat(gres[f, at])
-            gx_ref[0, f, at] = tall(out.astype(jnp.bfloat16))
-            return carry
-
-        lax.fori_loop(0, cuts, body, 0)
+        for starts, count in inside + [border]:
+            own = [gres[f, pl.ds(y, count)].reshape(count * width, ch) for y in starts]
+            out = conv(gp, f, starts, count, wb) + jnp.concatenate(own, axis=0)
+            spread(gx_ref.at[0], f, starts, count, out.astype(jnp.bfloat16))
 
     features(0)
     small.start()
@@ -456,6 +471,7 @@
             pltpu.VMEM(frame, bf),
             pltpu.VMEM(frame, bf),
             pltpu.VMEM((4,) + frame, bf),
+            pltpu.VMEM((3 * ch, rows * width), bf),
             pltpu.VMEM(frame, f32),
             pltpu.VMEM(frame, bf),
             pltpu.VMEM(frame, bf),

time: 34.6 us -> 35.1 us (1.014)
  Pallas kernels: 33.9 us -> 34.3 us
    pallas_call x1, Pallas kernels: 32.6 us -> 33.1 us  [per_device(): pl.pallas_call(functools.partial(kernel, dims, step), out_shape=shapes, i...]
where the time goes in v5:
time: 35.1 us; the launch traced here: 35 us
  Pallas kernels  34.3 us (98%)
  between operations  0.64 us (2%)
    pallas_call x1, Pallas kernels, per_device(): pl.pallas_call(functools.partial(kernel, dims, step), out_shape=shapes, i...  33.1 us
    pallas_call x1, Pallas kernels, per_device(): pl.pallas_call(store, out_shape=shapes, in_specs=[pl.BlockSpec(memory_spa...  1.24 us

profile of v5, /device:TPU:0, one launch (start us, length us, event | category | flops | bytes accessed | tf_op | source)
XLA Modules:
  0.0 35.0 jit_solution(17728822635747346457)
XLA Ops:
  0.6 33.1 %shard_map.92 = (bf16[1,1,8,128,128]{4,3,2,1,0:T(8,128)(2,1)S(1)}, bf16[1,2,8,128,128]{4,3,2,1,0:T(8,128)(2,1)S(1)}, f32[3,3,128,128]{3,2,1,0:T(8,128)S(1)}, f32...) custom-call(bf16[1,2,8,128,128]{4,3,2,1,0:T(8,128)(2,1)} %x_hbm.1, bf16[3,3,128,128]{3,2,1,0:T(8,128)(2,1)} %ws_hbm.1, ...), custom_call_target="tpu_custom_call" | custom-call | tf_op jit(solution)/shard_map/pallas_call | solution.py:457
  33.7 1.2 %shard_map.93 = (bf16[1,1,8,128,128]{4,3,2,1,0:T(8,128)(2,1)}, bf16[1,2,8,128,128]{4,3,2,1,0:T(8,128)(2,1)}, f32[3,3,128,128]{3,2,1,0:T(8,128)}, f32[3,128,128]{2,1,0:T(8,128)}, f32[3,128,128]{2,1,0:T(8,128)}) custom-call(bf16[1,1,8,128,128]{4,3,2,1,0:T(8,128)(2,1)S(1)} %get-tuple-element.10.refs_0_, ...), custom_call_target="tpu_custom_call" | custom-call | tf_op jit(solution)/shard_map/pallas_call | solution.py:499

commit v6 on v5

--- a/solution.py
+++ b/solution.py
@@ -125,10 +125,12 @@
             self.gather(o).start()
         self.forward(0).start()
 
-    def finish(self):
+    def relay(self):
         for o in range(1, self.chips):
             self.gather(o).wait()
             self.forward(o).start()
+
+    def finish(self):
         for o in range(self.chips):
             self.forward(o).wait()
 
@@ -327,8 +329,6 @@
         return carry
 
     lax.fori_loop(0, cuts, mixing, 0)
-    for e in edges[4:]:
-        e.start()
 
     ct[ch : 2 * ch, :] = c_ref[0, 0].reshape(tokens, ch).T
 
@@ -356,6 +356,9 @@
     for i in range(cuts):
         for e in near[i]:
             e.arrive()
+        if i == cuts - 1:
+            for e in edges[4:]:
+                e.start()
         backward(i)
     for e in edges[2:4]:
         e.start()
@@ -416,9 +419,11 @@
         part[...] + d_in[...].astype(jnp.float32) + e_in[...].astype(jnp.float32)
     ).astype(jnp.bfloat16)
     small.last()
+    big.relay()
     big.finish()
     for i in range(9):
         os_ref[i // 3, i % 3] = big.full[pl.ds(i * ch, ch)].astype(jnp.float32)
+    small.relay()
     small.finish()
     for i in range(3):
         ot_ref[i] = small.full[pl.ds(i * ch, ch)].astype(jnp.float32)

time: 35.1 us -> 34.7 us (0.989)
  Pallas kernels: 34.3 us -> 33.9 us
    pallas_call x1, Pallas kernels: 33.1 us -> 32.6 us  [per_device(): pl.pallas_call(functools.partial(kernel, dims, step), out_shape=shapes, i...]
where the time goes in v6:
time: 34.7 us; the launch traced here: 34.5 us
  Pallas kernels  33.9 us (98%)
  between operations  0.64 us (2%)
    pallas_call x1, Pallas kernels, per_device(): pl.pallas_call(functools.partial(kernel, dims, step), out_shape=shapes, i...  32.6 us
    pallas_call x1, Pallas kernels, per_device(): pl.pallas_call(store, out_shape=shapes, in_specs=[pl.BlockSpec(memory_spa...  1.24 us

profile of v6, /device:TPU:0, one launch (start us, length us, event | category | flops | bytes accessed | tf_op | source)
XLA Modules:
  0.0 34.5 jit_solution(853138628995233205)
XLA Ops:
  0.6 32.6 %shard_map.92 = (bf16[1,1,8,128,128]{4,3,2,1,0:T(8,128)(2,1)S(1)}, bf16[1,2,8,128,128]{4,3,2,1,0:T(8,128)(2,1)S(1)}, f32[3,3,128,128]{3,2,1,0:T(8,128)S(1)}, f32...) custom-call(bf16[1,2,8,128,128]{4,3,2,1,0:T(8,128)(2,1)} %x_hbm.1, bf16[3,3,128,128]{3,2,1,0:T(8,128)(2,1)} %ws_hbm.1, ...), custom_call_target="tpu_custom_call" | custom-call | tf_op jit(solution)/shard_map/pallas_call | solution.py:462
  33.3 1.2 %shard_map.93 = (bf16[1,1,8,128,128]{4,3,2,1,0:T(8,128)(2,1)}, bf16[1,2,8,128,128]{4,3,2,1,0:T(8,128)(2,1)}, f32[3,3,128,128]{3,2,1,0:T(8,128)}, f32[3,128,128]{2,1,0:T(8,128)}, f32[3,128,128]{2,1,0:T(8,128)}) custom-call(bf16[1,1,8,128,128]{4,3,2,1,0:T(8,128)(2,1)S(1)} %get-tuple-element.10.refs_0_, ...), custom_call_target="tpu_custom_call" | custom-call | tf_op jit(solution)/shard_map/pallas_call | solution.py:504

commit v7 on v6

--- a/solution.py
+++ b/solution.py
@@ -380,7 +380,8 @@
     for a in range(2):
         wide = jnp.concatenate([gb[n].reshape(tokens, ch) for n in (a + 2, a + 1, a)], axis=1)
         times = times + dot(act[a].reshape(tokens, ch).T, wide)
-    big.start()
+        if a == 0:
+            big.start()
     ct[0:ch, :] = cp[...].reshape(tokens, ch).T
     ct[2 * ch :, :] = cm[...].reshape(tokens, ch).T
     wide = jnp.concatenate([lcat[n].reshape(tokens, ch) for n in range(4)], axis=1)
@@ -394,6 +395,7 @@
         small.out[pl.ds(k * ch, ch)] = times[:, k * ch : (k + 1) * ch]
         small.out[pl.ds((3 + k) * ch, ch)] = downs[k].T
     small.pair()
+    big.middle()
     for dy in range(3):
         for dx in range(3):
             at = slice((2 - dy) * ch, (3 - dy) * ch), slice((2 - dx) * ch, (3 - dx) * ch)
@@ -409,7 +411,6 @@
 
     features(0)
     small.start()
-    big.middle()
     features(1)
     small.middle()
     big.last()

time: 34.7 us -> 35.6 us (1.026)
  Pallas kernels: 33.9 us -> 34.8 us
    pallas_call x1, Pallas kernels: 32.6 us -> 33.5 us  [per_device(): pl.pallas_call(functools.partial(kernel, dims, step), out_shape=shapes, i...]
where the time goes in v7:
time: 35.6 us; the launch traced here: 35.4 us
  Pallas kernels  34.8 us (98%)
  between operations  0.64 us (2%)
    pallas_call x1, Pallas kernels, per_device(): pl.pallas_call(functools.partial(kernel, dims, step), out_shape=shapes, i...  33.5 us
    pallas_call x1, Pallas kernels, per_device(): pl.pallas_call(store, out_shape=shapes, in_specs=[pl.BlockSpec(memory_spa...  1.24 us

profile of v7, /device:TPU:0, one launch (start us, length us, event | category | flops | bytes accessed | tf_op | source)
XLA Modules:
  0.0 35.4 jit_solution(15368471139096860053)
XLA Ops:
  0.6 33.5 %shard_map.92 = (bf16[1,1,8,128,128]{4,3,2,1,0:T(8,128)(2,1)S(1)}, bf16[1,2,8,128,128]{4,3,2,1,0:T(8,128)(2,1)S(1)}, f32[3,3,128,128]{3,2,1,0:T(8,128)S(1)}, f32...) custom-call(bf16[1,2,8,128,128]{4,3,2,1,0:T(8,128)(2,1)} %x_hbm.1, bf16[3,3,128,128]{3,2,1,0:T(8,128)(2,1)} %ws_hbm.1, ...), custom_call_target="tpu_custom_call" | custom-call | tf_op jit(solution)/shard_map/pallas_call | solution.py:463
  34.2 1.2 %shard_map.93 = (bf16[1,1,8,128,128]{4,3,2,1,0:T(8,128)(2,1)}, bf16[1,2,8,128,128]{4,3,2,1,0:T(8,128)(2,1)}, f32[3,3,128,128]{3,2,1,0:T(8,128)}, f32[3,128,128]{2,1,0:T(8,128)}, f32[3,128,128]{2,1,0:T(8,128)}) custom-call(bf16[1,1,8,128,128]{4,3,2,1,0:T(8,128)(2,1)S(1)} %get-tuple-element.10.refs_0_, ...), custom_call_target="tpu_custom_call" | custom-call | tf_op jit(solution)/shard_map/pallas_call | solution.py:505
